TPU v7x, 256 devices: a whole 4x4x8 slice. The times are simulated.
256 devices in a mesh: row: 32 (over z, x_lo, core), col: 8 (over y, x_hi).
Axes of the slice: x: 4 (x_hi: 2, x_lo: 2; x = x_hi * 2 + x_lo), y: 4, z: 8, core: 2. Of those that a mesh axis runs over, the one named last changes fastest.
Arguments:
- x_feat: bfloat16 [16384, 256], P('row', 'col')
- y_feat: bfloat16 [24576, 256], P('col', 'row')
- a_logits: float32 [16384], P('row')
- b_logits: float32 [24576], P('col')
Outputs:
- f_potential: float32 [16384], P('row')
- g_potential: float32 [24576], P('col')
- loss: float32 [], replicated
All inputs are finite; a program needn't handle non-finite values.
Results may differ from a plain program's by a relative error of at most 0.0003.
Values may be sent and summed in bfloat16 or wider, within the bound.
A program may use at most 64 MiB of HBM per device.

v0:
```python
import jax
import jax.numpy as jnp
from jax import lax
from jax.sharding import PartitionSpec as P

ITERS = 4


epsilon = 0.05


def across_cols(row_peak, row_mass):
    whole_peak = lax.pmax(row_peak, "col")
    whole_mass = lax.psum(row_mass * jnp.exp(row_peak - whole_peak), "col")
    return (whole_peak, whole_mass)


def across_rows(col_peak, col_mass):
    whole_peak = lax.pmax(col_peak, "row")
    whole_mass = lax.psum(col_mass * jnp.exp(col_peak - whole_peak), "row")
    return (whole_peak, whole_mass)


def inner_rows(left, right):
    return lax.dot_general(
        left, right, (((1,), (1,)), ((), ())), preferred_element_type=jnp.float32
    )


def body(x_feat, y_feat, a_logits, b_logits):
    x_rows = lax.all_gather(x_feat, "col", axis=1, tiled=True)
    width = x_rows.shape[1]
    row_count = x_rows.shape[0]
    col_count = b_logits.shape[0]
    cols_block = 512
    block_count = col_count // cols_block
    x_float = x_rows.astype(jnp.float32)
    x_square = jnp.sum(x_float * x_float, axis=1)
    a_peak = jnp.max(a_logits)
    a_total = across_rows(a_peak[None], jnp.sum(jnp.exp(a_logits - a_peak))[None])
    log_a = a_logits - (a_total[0] + jnp.log(a_total[1]))[0]
    b_peak = jnp.max(b_logits)
    b_total = across_cols(b_peak[None], jnp.sum(jnp.exp(b_logits - b_peak))[None])
    log_b = b_logits - (b_total[0] + jnp.log(b_total[1]))[0]
    y_cols = lax.all_gather(y_feat, "row", axis=1, tiled=True)
    y_float = y_cols.astype(jnp.float32)
    y_square = jnp.sum(y_float * y_float, axis=1)

    def get_tile(index):
        y_block = lax.dynamic_slice_in_dim(y_cols, index * cols_block, cols_block, 0)
        ys_block = lax.dynamic_slice_in_dim(y_square, index * cols_block, cols_block, 0)
        return (x_square[:, None] + ys_block[None, :] - 2.0 * inner_rows(x_rows, y_block)) / width

    indices = jnp.arange(block_count, dtype=jnp.int32)
    potential_g = jnp.zeros((col_count,), jnp.float32)
    potential_f = jnp.zeros((row_count,), jnp.float32)
    for step in range(ITERS):

        def row_step(carry, index):
            row_peak, row_mass = carry
            cost_tile = get_tile(index)
            g_part = lax.dynamic_slice_in_dim(potential_g, index * cols_block, cols_block, 0)
            lb_part = lax.dynamic_slice_in_dim(log_b, index * cols_block, cols_block, 0)
            scores = lb_part[None, :] + (g_part[None, :] - cost_tile) / epsilon
            new_peak = jnp.maximum(row_peak, jnp.max(scores, axis=1))
            new_mass = row_mass * jnp.exp(row_peak - new_peak) + jnp.sum(
                jnp.exp(scores - new_peak[:, None]), axis=1
            )
            return ((new_peak, new_mass), None)

        start_rows = (
            jnp.full((row_count,), -jnp.inf, jnp.float32),
            jnp.zeros((row_count,), jnp.float32),
        )
        (row_peak, row_mass), unused = lax.scan(row_step, start_rows, indices)
        whole_peak, whole_mass = across_cols(row_peak, row_mass)
        potential_f = -epsilon * (whole_peak + jnp.log(whole_mass))

        def col_step(carry, index):
            cost_tile = get_tile(index)
            scores = log_a[:, None] + (potential_f[:, None] - cost_tile) / epsilon
            col_peak = jnp.max(scores, axis=0)
            col_mass = jnp.sum(jnp.exp(scores - col_peak[None, :]), axis=0)
            return (carry, (col_peak, col_mass))

        unused, (col_peak, col_mass) = lax.scan(col_step, 0, indices)
        whole_peak, whole_mass = across_rows(
            col_peak.reshape(col_count), col_mass.reshape(col_count)
        )
        potential_g = -epsilon * (whole_peak + jnp.log(whole_mass))
    share = jnp.sum(jnp.exp(log_a) * potential_f) / lax.axis_size("col") + jnp.sum(
        jnp.exp(log_b) * potential_g
    ) / lax.axis_size("row")
    loss = lax.psum(share, ("row", "col"))
    return (potential_f, potential_g, loss)


def solution(mesh):
    in_specs = (P("row", "col"), P("col", "row"), P("row"), P("col"))
    out_specs = (P("row"), P("col"), P())
    return jax.shard_map(body, mesh=mesh, in_specs=in_specs, out_specs=out_specs, check_vma=False)
```

profile of v0, /device:TPU:1, one launch (start us, length us, event | category | flops | bytes accessed | tf_op | source)
XLA Modules:
  0.0 1407.0 jit_solution(8104502084648880321)
XLA Ops:
  9.2 22.3 %pmax.70 = f32[1]{0:T(128)} all-reduce(f32[1]{0:T(128)} %bitcast.16), channel_id=1, replica_groups=mesh['row'=32,'col'=8] {'col'}, use_global_device_ids=true, to_apply=%region_7.0 | all-reduce | flops 1 | bytes 8 | tf_op jit(solution)/shard_map/pmax | solution.py:13
  32.8 59.7 %pmax.71 = f32[1]{0:T(128)} all-reduce(f32[1]{0:T(128)} %bitcast.19), channel_id=1, replica_groups=mesh['row'=32,'col'=8] {'row'}, use_global_device_ids=true, to_apply=%region_3.0 | all-reduce | flops 1 | bytes 8 | tf_op jit(solution)/shard_map/pmax | solution.py:19
  100.3 16.1 %psum.77 = f32[1]{0:T(128)} all-reduce(f32[1]{0:T(128)S(6)} %mul.189), channel_id=1, replica_groups=mesh['row'=32,'col'=8] {'col'}, use_global_device_ids=true, to_apply=%region_9.0 | all-reduce | flops 1 | bytes 8 | tf_op jit(solution)/shard_map/psum | solution.py:14
  116.4 56.8 %psum.78 = f32[1]{0:T(128)} all-reduce(f32[1]{0:T(128)S(6)} %mul.190), channel_id=1, replica_groups=mesh['row'=32,'col'=8] {'row'}, use_global_device_ids=true, to_apply=%region_5.0 | all-reduce | flops 1 | bytes 8 | tf_op jit(solution)/shard_map/psum | solution.py:20
  175.8 29.1 %all_gather.6 = bf16[512,256]{0,1:T(8,128)(2,1)S(1)} all-gather(bf16[512,32]{0,1:T(8,128)(2,1)} %param.20), channel_id=1, replica_groups=mesh['row'=32,'col'=8] {'col'}, dimensions={1}, use_global_device_ids=true | all-gather | bytes 294912 | tf_op jit(solution)/shard_map/all_gather | solution.py:31
  221.8 18.7 %pmax.72 = f32[512]{0:T(512)S(1)} all-reduce(f32[512]{0:T(512)S(1)} %get-tuple-element.422), channel_id=1, replica_groups=mesh['row'=32,'col'=8] {'col'}, use_global_device_ids=true, to_apply=%region_14.15 | all-reduce | flops 512 | bytes 4096 | tf_op jit(solution)/shard_map/pmax | solution.py:13
  240.5 16.0 %psum.79 = f32[512]{0:T(512)S(1)} all-reduce(f32[512]{0:T(512)S(1)} %exponential_multiply_fusion.7), channel_id=1, replica_groups=mesh['row'=32,'col'=8] {'col'}, use_global_device_ids=true, to_apply=%region_15.16 | all-reduce | flops 512 | bytes 4096 | tf_op jit(solution)/shard_map/psum | solution.py:14
  256.5 13.7 while.100
  270.3 113.5 %pmax.73 = f32[3072]{0:T(1024)S(1)} all-reduce(f32[3072]{0:T(1024)S(1)} %reshape.85), channel_id=1, replica_groups=mesh['row'=32,'col'=8] {'row'}, use_global_device_ids=true, to_apply=%region_20.21 | all-reduce | flops 3072 | bytes 24576 | tf_op jit(solution)/shard_map/pmax | solution.py:19
  383.7 104.4 %psum.80 = f32[3072]{0:T(1024)S(1)} all-reduce(f32[3072]{0:T(1024)S(1)} %exponential_multiply_fusion.3), channel_id=1, replica_groups=mesh['row'=32,'col'=8] {'row'}, use_global_device_ids=true, to_apply=%region_21.22 | all-reduce | flops 3072 | bytes 24576 | tf_op jit(solution)/shard_map/psum | solution.py:20
  488.2 13.5 while.105
  501.7 18.5 %pmax.74 = f32[512]{0:T(512)S(1)} all-reduce(f32[512]{0:T(512)S(1)} %get-tuple-element.426), channel_id=1, replica_groups=mesh['row'=32,'col'=8] {'col'}, use_global_device_ids=true, to_apply=%region_26.27 | all-reduce | flops 512 | bytes 4096 | tf_op jit(solution)/shard_map/pmax | solution.py:13
  520.2 15.9 %psum.81 = f32[512]{0:T(512)S(1)} all-reduce(f32[512]{0:T(512)S(1)} %exponential_multiply_fusion.6), channel_id=1, replica_groups=mesh['row'=32,'col'=8] {'col'}, use_global_device_ids=true, to_apply=%region_27.28 | all-reduce | flops 512 | bytes 4096 | tf_op jit(solution)/shard_map/psum | solution.py:14
  549.2 111.6 %pmax.75 = f32[3072]{0:T(1024)S(1)} all-reduce(f32[3072]{0:T(1024)S(1)} %reshape.87), channel_id=1, replica_groups=mesh['row'=32,'col'=8] {'row'}, use_global_device_ids=true, to_apply=%region_32.33 | all-reduce | flops 3072 | bytes 24576 | tf_op jit(solution)/shard_map/pmax | solution.py:19
  660.8 104.4 %psum.82 = f32[3072]{0:T(1024)S(1)} all-reduce(f32[3072]{0:T(1024)S(1)} %exponential_multiply_fusion.2), channel_id=1, replica_groups=mesh['row'=32,'col'=8] {'row'}, use_global_device_ids=true, to_apply=%region_33.34 | all-reduce | flops 3072 | bytes 24576 | tf_op jit(solution)/shard_map/psum | solution.py:20
  778.5 18.5 %pmax.76 = f32[512]{0:T(512)S(1)} all-reduce(f32[512]{0:T(512)S(1)} %get-tuple-element.430), channel_id=1, replica_groups=mesh['row'=32,'col'=8] {'col'}, use_global_device_ids=true, to_apply=%region_38.39 | all-reduce | flops 512 | bytes 4096 | tf_op jit(solution)/shard_map/pmax | solution.py:13
  797.0 15.9 %psum.83 = f32[512]{0:T(512)S(1)} all-reduce(f32[512]{0:T(512)S(1)} %exponential_multiply_fusion.5), channel_id=1, replica_groups=mesh['row'=32,'col'=8] {'col'}, use_global_device_ids=true, to_apply=%region_39.40 | all-reduce | flops 512 | bytes 4096 | tf_op jit(solution)/shard_map/psum | solution.py:14
  825.8 111.6 %pmax.77 = f32[3072]{0:T(1024)S(1)} all-reduce(f32[3072]{0:T(1024)S(1)} %reshape.89), channel_id=1, replica_groups=mesh['row'=32,'col'=8] {'row'}, use_global_device_ids=true, to_apply=%region_44.45 | all-reduce | flops 3072 | bytes 24576 | tf_op jit(solution)/shard_map/pmax | solution.py:19
  937.5 104.4 %psum.84 = f32[3072]{0:T(1024)S(1)} all-reduce(f32[3072]{0:T(1024)S(1)} %exponential_multiply_fusion.1), channel_id=1, replica_groups=mesh['row'=32,'col'=8] {'row'}, use_global_device_ids=true, to_apply=%region_45.46 | all-reduce | flops 3072 | bytes 24576 | tf_op jit(solution)/shard_map/psum | solution.py:20
  1055.2 18.5 %pmax.78 = f32[512]{0:T(512)S(1)} all-reduce(f32[512]{0:T(512)S(1)} %get-tuple-element.434), channel_id=1, replica_groups=mesh['row'=32,'col'=8] {'col'}, use_global_device_ids=true, to_apply=%region_50.51 | all-reduce | flops 512 | bytes 4096 | tf_op jit(solution)/shard_map/pmax | solution.py:13
  1073.7 15.9 %psum.85 = f32[512]{0:T(512)S(1)} all-reduce(f32[512]{0:T(512)S(1)} %exponential_multiply_fusion.4), channel_id=1, replica_groups=mesh['row'=32,'col'=8] {'col'}, use_global_device_ids=true, to_apply=%region_51.52 | all-reduce | flops 512 | bytes 4096 | tf_op jit(solution)/shard_map/psum | solution.py:14
  1103.3 111.6 %pmax.79 = f32[3072]{0:T(1024)S(1)} all-reduce(f32[3072]{0:T(1024)S(1)} %reshape.91), channel_id=1, replica_groups=mesh['row'=32,'col'=8] {'row'}, use_global_device_ids=true, to_apply=%region_56.57 | all-reduce | flops 3072 | bytes 24576 | tf_op jit(solution)/shard_map/pmax | solution.py:19
  1214.9 104.4 %psum.86 = f32[3072]{0:T(1024)S(1)} all-reduce(f32[3072]{0:T(1024)S(1)} %exponential_multiply_fusion), channel_id=1, replica_groups=mesh['row'=32,'col'=8] {'row'}, use_global_device_ids=true, to_apply=%region_57.58 | all-reduce | flops 3072 | bytes 24576 | tf_op jit(solution)/shard_map/psum | solution.py:20
  1321.9 78.3 %psum.87 = f32[]{:T(128)} all-reduce(f32[]{:T(128)S(6)} %add.308), channel_id=1, replica_groups=mesh['row'=32,'col'=8] {'row','col'}, use_global_device_ids=true, to_apply=%region_60.61 | all-reduce | flops 1 | bytes 8 | tf_op jit(solution)/shard_map/psum | solution.py:94
  (429 shorter events, 163.9 us)
Async XLA Ops:
  7.2 199.4 %all-gather.2.cloned.1.call-start = ((), (), s32[]{:S(2)}) async-start(), calls=%async_computation | async-start | bytes 1622016 | tf_op jit(solution)/shard_map/all_gather | solution.py:45
  206.5 1.9 copy-start
  1041.9 47.6 %copy-start.2 = (f32[512]{0:T(512)S(1)}, f32[512]{0:T(512)}, u32[]{:S(2)}) copy-start(f32[512]{0:T(512)} %param.22) | copy-start | bytes 6148
  1090.3 229.1 %copy-start.1 = (f32[3072]{0:T(1024)S(1)}, f32[3072]{0:T(1024)}, u32[]{:S(2)}) copy-start(f32[3072]{0:T(1024)} %param.23) | copy-start | bytes 36868
  1103.2 297.0 %copy-start.3 = (f32[512]{0:T(512)}, f32[512]{0:T(512)S(1)}, u32[]{:S(2)}) copy-start(f32[512]{0:T(512)S(1)} %get-tuple-element.1709) | copy-start | bytes 6148
Sparse Core Ops, SparseCore 0:
  9.9 68.4 all-gather.1
where the time goes:
time: 1410 us
  blocking collectives  1270 us (90%)
  local copies, waits for them, and re-layouts  39.9 us (3%)
  loops' own time  32.9 us (2%)
  matrix products  23.4 us (2%)
  between operations  22.1 us (2%)
  other arithmetic  21.9 us (2%)
    pmax x5, blocking collectives, across_rows(): whole_peak = lax.pmax(col_peak, 'row')  508 us
    psum x5, blocking collectives, across_rows(): whole_mass = lax.psum(col_mass * jnp.exp(col_peak - whole_peak), 'row')  474 us
    pmax x5, blocking collectives, across_cols(): whole_peak = lax.pmax(row_peak, 'col')  96.5 us
    psum x5, blocking collectives, across_cols(): whole_mass = lax.psum(row_mass * jnp.exp(row_peak - whole_peak), 'col')  79.7 us
    psum x1, blocking collectives, body(): loss = lax.psum(share, ('row', 'col'))  78.3 us
    dynamic_slice x48, local copies, waits for them, and re-layouts, body(): (row_peak, row_mass), unused = lax.scan(row_step, start_rows, indices)  29.3 us
    all_gather x1, blocking collectives, body(): x_rows = lax.all_gather(x_feat, 'col', axis=1, tiled=True)  29.1 us
  transfers between devices with their start and end apart: 1, of which 0 were waited for; matrix products, arithmetic and copies ran while one was open for 1% of the time, Pallas kernels for 0%

commit v1 on v0

v1 whole, which is shorter than its diff:
```python
import functools
import math

import jax
import jax.numpy as jnp
from jax import lax
from jax.experimental import pallas as pl
from jax.experimental.pallas import tpu as pltpu
from jax.sharding import PartitionSpec as P

ITERS = 4
EPS = 0.05
LN2 = math.log(2.0)
LOG2E = 1.0 / LN2
F = 256
SIZE = {"z": 8, "xl": 2, "c": 2, "y": 4, "xh": 2}
MESH = pl.DeviceIdType.MESH
ROWS, COLS = 1024, 1536
KT = COLS // 128


def coords():
    r = lax.axis_index("row")
    k = lax.axis_index("col")
    return {"z": r // 4, "xl": lax.rem(r // 2, 2), "c": lax.rem(r, 2), "y": k // 2, "xh": lax.rem(k, 2)}


def device(o):
    return ((o["z"] * 2 + o["xl"]) * 2 + o["c"], o["y"] * 2 + o["xh"])


def hops(o):
    z, y = o.get("z", 0), o.get("y", 0)
    return min(z, 8 - z) + min(y, 4 - y) + 2 * o.get("xh", 0) + o.get("xl", 0)


def offsets(names):
    out = [{}]
    for n in names:
        out = [{**o, n: d} for o in out for d in range(SIZE[n])]
    return sorted([o for o in out if any(o.values())], key=lambda o: -hops(o))


def at_offset(co, o):
    return {n: (lax.rem(co[n] + o[n], SIZE[n]) if o.get(n, 0) else co[n]) for n in co}


def send(src, dst, ssem, rsem, target):
    pltpu.make_async_remote_copy(
        src_ref=src, dst_ref=dst, send_sem=ssem, recv_sem=rsem, device_id=device(target), device_id_type=MESH
    ).start()


def drain(ref, sem):
    pltpu.make_async_copy(ref, ref, sem).wait()


def lse(x):
    peak = jnp.max(x, axis=0)
    return peak + jnp.log2(jnp.sum(jnp.exp2(x - peak[None]), axis=0))


def full_lse(x):
    peak = jnp.max(x, axis=(0, 1), keepdims=True)
    return peak + jnp.log2(jnp.sum(jnp.exp2(x - peak), axis=(0, 1), keepdims=True))


def kernel(
    xt, yt, a, b, f_out, g_out, loss_out,
    XT, Y8, YM, S, VB, UB, ALL_A, ALL_B, LA, LB, XSQ, YSQ, GM, GS, FX, GX, FL, GL, GH,
    ysem, xsem, asem, bsem, csem, local, fs, fr, gs, gr, ends,
):
    co = coords()
    row, col = device(co)
    zx = co["z"] * 2 + co["xl"]
    xy = (co["xh"] * 2 + co["xl"]) * 4 + co["y"]
    zc = co["z"] * 2 + co["c"]
    xy_peers = [at_offset(co, o) for o in offsets(["y", "xh", "xl"])]
    zc_peers = [at_offset(co, o) for o in offsets(["z", "c"])]
    zx_peers = [at_offset(co, o) for o in offsets(["z", "xl"])]
    row_peers = [at_offset(co, o) for o in offsets(["z", "xl", "c"])]
    col_peers = [at_offset(co, o) for o in offsets(["y", "xh"])]
    barrier_peers = row_peers + [at_offset(co, o) for o in offsets(["y", "xh", "xl"]) if o.get("y", 0) or o.get("xh", 0)]
    sibling = at_offset(co, {"c": 1})

    barrier = pltpu.get_barrier_semaphore()
    for t in barrier_peers:
        pl.semaphore_signal(barrier, inc=1, device_id=device(t), device_id_type=MESH)

    own_x = pltpu.make_async_copy(xt, XT.at[co["xl"] * 8 + col], local.at[0])
    own_x.start()
    half = pl.ds(pl.multiple_of(co["xl"] * COLS, 128), COLS)
    own_y = pltpu.make_async_copy(yt.at[:, half], Y8.at[co["c"], zx], local.at[1])
    own_y.start()
    ALL_A[row] = a[...]
    ALL_B[col] = b[...]
    pl.semaphore_wait(barrier, len(barrier_peers))

    for ty, tx in zip(zx_peers, xy_peers):
        part = pl.ds(pl.multiple_of(ty["xl"] * COLS, 128), COLS)
        send(yt.at[:, part], Y8.at[co["c"], zx], ysem.at[0], ysem.at[1], ty)
        send(xt, XT.at[co["xl"] * 8 + col], xsem.at[0], xsem.at[1], tx)
    for t in row_peers:
        send(ALL_A.at[row], ALL_A.at[row], asem.at[0], asem.at[1], t)
    for t in col_peers:
        send(ALL_B.at[col], ALL_B.at[col], bsem.at[0], bsem.at[1], t)

    own_x.wait()
    own_y.wait()
    drain(Y8.at[0, pl.ds(0, 15)], ysem.at[1])
    send(Y8.at[co["c"]], Y8.at[co["c"]], csem.at[0], csem.at[1], sibling)

    drain(ALL_A.at[pl.ds(0, 31)], asem.at[1])
    drain(ALL_B.at[pl.ds(0, 7)], bsem.at[1])
    whole_a = ALL_A[...].reshape(128, 128) * LOG2E
    log_a_norm = full_lse(whole_a)
    mine = jnp.concatenate([ALL_A[co["z"] * 4 + co["c"]], ALL_A[co["z"] * 4 + 2 + co["c"]]], axis=0)
    LA[...] = mine * LOG2E - log_a_norm
    whole_b = ALL_B[...].reshape(192, 128) * LOG2E
    log_b_norm = full_lse(whole_b)
    b_all = b[...]
    LB[...] = jnp.where(co["xl"] == 0, b_all[:KT], b_all[KT:]) * LOG2E - log_b_norm
    drain(XT.at[pl.ds(0, 15)], xsem.at[1])
    for p in range(8):
        x = XT[p // 4 * 8 : p // 4 * 8 + 8, :, pl.ds((p % 4) * 128, 128)].astype(jnp.float32).reshape(F, 128)
        XSQ[p : p + 1, :] = jnp.sum(x * x, axis=0, keepdims=True)
    drain(Y8.at[0], csem.at[1])

    def assemble(q, total):
        y = jnp.concatenate([Y8[0, q].astype(jnp.float32), Y8[1, q].astype(jnp.float32)], axis=0)
        YM[pl.ds(pl.multiple_of(q * 16, 16), 16), :] = y.astype(jnp.bfloat16)
        return total + y * y

    total = lax.fori_loop(0, 16, assemble, jnp.zeros((16, COLS), jnp.float32))
    total = jnp.sum(total, axis=0, keepdims=True)
    for k in range(KT):
        YSQ[k : k + 1, :] = total[:, k * 128 : (k + 1) * 128]

    scale = 2.0 / F / EPS * LOG2E
    for p in range(8):
        x = XT[p // 4 * 8 : p // 4 * 8 + 8, :, pl.ds((p % 4) * 128, 128)].reshape(F, 128)
        inner = lax.dot_general(x, YM[...], (((0,), (0,)), ((), ())), preferred_element_type=jnp.float32)
        S[pl.ds(p * 128, 128), :] = inner * scale

    def set_v(v):
        for k in range(KT):
            VB[:, k * 128 : (k + 1) * 128] = jnp.broadcast_to(v[k : k + 1, :], (8, 128))

    set_v(LB[...] - YSQ[...] * (LOG2E / F / EPS))

    def exchange(buf, me, peers, ssem, rsem):
        for t in peers:
            send(buf.at[me], buf.at[me], ssem, rsem, t)
        drain(buf.at[pl.ds(0, 15)], ssem)
        drain(buf.at[pl.ds(0, 15)], rsem)

    def iteration(t, _):
        def row_block(p, _):
            peaks, masses = [], []
            for r in range(16):
                at = pl.ds(pl.multiple_of(p * 128 + r * 8, 8), 8)
                tiles = [S[at, k * 128 : (k + 1) * 128] + VB[:, k * 128 : (k + 1) * 128] for k in range(KT)]
                peak = functools.reduce(jnp.maximum, tiles)
                peaks.append(peak)
                masses.append(functools.reduce(jnp.add, [jnp.exp2(s - peak) for s in tiles]))
            peak = jnp.concatenate(peaks, axis=0).T
            mass = jnp.concatenate(masses, axis=0).T
            top = jnp.max(peak, axis=0, keepdims=True)
            mass = jnp.sum(mass * jnp.exp2(peak - top), axis=0, keepdims=True)
            FX[t, xy, pl.ds(p, 1), :] = top + jnp.log2(mass)
            return 0

        lax.fori_loop(0, 8, row_block, 0)
        exchange(FX.at[t], xy, xy_peers, fs.at[t], fr.at[t])
        u = LA[...] - lse(FX[t])
        for p in range(8):
            UB[pl.ds(p * 128, 128), :] = jnp.broadcast_to(u[p : p + 1, :], (128, 128)).T

        def col_block(i, carry):
            peaks, masses = carry
            us = [UB[pl.ds(pl.multiple_of(i * 64 + r * 8, 8), 8), :] for r in range(8)]
            new_peaks, new_masses = [], []
            for k in range(KT):
                tiles = [
                    S[pl.ds(pl.multiple_of(i * 64 + r * 8, 8), 8), k * 128 : (k + 1) * 128] + us[r] for r in range(8)
                ]
                peak = functools.reduce(jnp.maximum, tiles + [peaks[k]])
                mass = functools.reduce(jnp.add, [jnp.exp2(s - peak) for s in tiles])
                new_masses.append(mass + masses[k] * jnp.exp2(peaks[k] - peak))
                new_peaks.append(peak)
            return new_peaks, new_masses

        start = [jnp.full((8, 128), -jnp.inf, jnp.float32)] * KT, [jnp.zeros((8, 128), jnp.float32)] * KT
        peaks, masses = lax.fori_loop(0, ROWS // 64, col_block, start)
        for k in range(KT):
            top = jnp.max(peaks[k], axis=0, keepdims=True)
            GM[k : k + 1, :] = top
            GS[k : k + 1, :] = jnp.sum(masses[k] * jnp.exp2(peaks[k] - top), axis=0, keepdims=True)
        GX[t, zc] = GM[...] + jnp.log2(GS[...])
        exchange(GX.at[t], zc, zc_peers, gs.at[t], gr.at[t])
        set_v(LB[...] - lse(GX[t]))
        return 0

    lax.fori_loop(0, ITERS, iteration, 0)
    last = ITERS - 1
    f = XSQ[...] * (1.0 / F) - lse(FX[last]) * (EPS * LN2)
    g = YSQ[...] * (1.0 / F) - lse(GX[last]) * (EPS * LN2)
    FL[zc] = jnp.exp2(LA[...]) * f
    GL[xy] = jnp.exp2(LB[...]) * g
    GH[co["xl"]] = g
    for t in xy_peers:
        send(GL.at[xy], GL.at[xy], ends.at[0], ends.at[1], t)
    send(GH.at[co["xl"]], GH.at[co["xl"]], ends.at[2], ends.at[3], at_offset(co, {"xl": 1}))
    for t in zc_peers:
        send(FL.at[zc], FL.at[zc], ends.at[4], ends.at[5], t)
    f_out[...] = jnp.where(co["xl"] == 0, f[:4], f[4:])
    drain(GH.at[0], ends.at[3])
    g_out[:KT] = GH[0]
    g_out[KT:] = GH[1]
    drain(GL.at[pl.ds(0, 15)], ends.at[1])
    drain(FL.at[pl.ds(0, 15)], ends.at[5])
    loss_out[...] = jnp.sum(jnp.sum(FL[...], axis=0), axis=(0, 1), keepdims=True) + jnp.sum(
        jnp.sum(GL[...], axis=0), axis=(0, 1), keepdims=True
    )
    drain(GL.at[pl.ds(0, 15)], ends.at[0])
    drain(GH.at[0], ends.at[2])
    drain(FL.at[pl.ds(0, 15)], ends.at[4])
    drain(Y8.at[0, pl.ds(0, 15)], ysem.at[0])
    drain(XT.at[pl.ds(0, 15)], xsem.at[0])
    drain(ALL_A.at[pl.ds(0, 31)], asem.at[0])
    drain(ALL_B.at[pl.ds(0, 7)], bsem.at[0])
    drain(Y8.at[0], csem.at[0])


def body(x_feat, y_feat, a_logits, b_logits):
    f32, bf16 = jnp.float32, jnp.bfloat16
    vmem = pl.BlockSpec(memory_space=pltpu.VMEM)
    hbm = pl.BlockSpec(memory_space=pl.ANY)
    dma = pltpu.SemaphoreType.DMA
    f, g, loss = pl.pallas_call(
        kernel,
        out_shape=(
            jax.ShapeDtypeStruct((4, 128), f32),
            jax.ShapeDtypeStruct((24, 128), f32),
            jax.ShapeDtypeStruct((1, 1), f32),
        ),
        in_specs=[hbm, hbm, vmem, vmem],
        out_specs=(vmem, vmem, vmem),
        scratch_shapes=[
            pltpu.VMEM((16, 32, 512), bf16),
            pltpu.VMEM((2, 16, 8, COLS), bf16),
            pltpu.VMEM((F, COLS), bf16),
            pltpu.VMEM((ROWS, COLS), f32),
            pltpu.VMEM((8, COLS), f32),
            pltpu.VMEM((ROWS, 128), f32),
            pltpu.VMEM((32, 4, 128), f32),
            pltpu.VMEM((8, 24, 128), f32),
            pltpu.VMEM((8, 128), f32),
            pltpu.VMEM((KT, 128), f32),
            pltpu.VMEM((8, 128), f32),
            pltpu.VMEM((KT, 128), f32),
            pltpu.VMEM((KT, 128), f32),
            pltpu.VMEM((KT, 128), f32),
            pltpu.VMEM((ITERS, 16, 8, 128), f32),
            pltpu.VMEM((ITERS, 16, KT, 128), f32),
            pltpu.VMEM((16, 8, 128), f32),
            pltpu.VMEM((16, KT, 128), f32),
            pltpu.VMEM((2, KT, 128), f32),
            dma((2,)),
            dma((2,)),
            dma((2,)),
            dma((2,)),
            dma((2,)),
            dma((2,)),
            dma((ITERS,)),
            dma((ITERS,)),
            dma((ITERS,)),
            dma((ITERS,)),
            dma((6,)),
        ],
        compiler_params=pltpu.CompilerParams(
            collective_id=0, has_side_effects=True, vmem_limit_bytes=40 * 1024 * 1024
        ),
        name="sinkhorn",
    )(x_feat.T, y_feat.T, a_logits.reshape(4, 128), b_logits.reshape(24, 128))
    return f.reshape(512), g.reshape(3072), loss.reshape(())


def solution(mesh):
    in_specs = (P("row", "col"), P("col", "row"), P("row"), P("col"))
    out_specs = (P("row"), P("col"), P())
    return jax.shard_map(body, mesh=mesh, in_specs=in_specs, out_specs=out_specs, check_vma=False)
```

time: 1410 us -> 91.9 us (0.07)
  blocking collectives: 1270 us -> 0 us
  Pallas kernels: 0 us -> 85.1 us
  local copies, waits for them, and re-layouts: 39.9 us -> 4.12 us
  loops' own time: 32.9 us -> 0 us
  matrix products: 23.4 us -> 0 us
  other arithmetic: 21.9 us -> 0 us
  between operations: 22.1 us -> 2.4 us
    psum x11 -> x0, blocking collectives: 632 us -> none  [the longest x5 474 us: across_rows(): whole_mass = lax.psum(col_mass * jnp.exp(col_peak - whole_peak), 'row')]
    pmax x10 -> x0, blocking collectives: 605 us -> none  [the longest x5 508 us: across_rows(): whole_peak = lax.pmax(col_peak, 'row')]
    pallas_call x0 -> x1, Pallas kernels: none -> 85.1 us  [body(): pl.pallas_call(kernel, out_shape=(jax.ShapeDtypeStruct((4, 128), f32), ja...]
    dynamic_slice x138 -> x0, local copies, waits for them, and re-layouts: 36.1 us -> none  [the longest x48 29.3 us: body(): (row_peak, row_mass), unused = lax.scan(row_step, start_rows, indices)]
    another operation x8 -> x0, loops' own time: 32.9 us -> none  [the longest x4 16.8 us: body(): unused, (col_peak, col_mass) = lax.scan(col_step, 0, indices)]
    all_gather x1 -> x0, blocking collectives: 29.1 us -> none  [body(): x_rows = lax.all_gather(x_feat, 'col', axis=1, tiled=True)]
    dot_general x48 -> x0, matrix products: 23.4 us -> none  [inner_rows(): lax.dot_general(left, right, (((1,), (1,)), ((), ())), preferred_element_...]
    reduce_sum x54 -> x0, other arithmetic: 17.2 us -> none  [the longest x24 4.74 us: col_step(): col_mass = jnp.sum(jnp.exp(scores - col_peak[None, :]), axis=0)]
  transfers between devices with their start and end apart: 1 -> 0, of which waited for: 0 -> 0; matrix products, arithmetic and copies ran while one was open for 1% -> 0% of each run, Pallas kernels for 0% -> 0%
where the time goes in v1:
time: 91.9 us; the launch traced here: 91.6 us
  Pallas kernels  85.1 us (93%)
  local copies, waits for them, and re-layouts  4.12 us (4%)
  between operations  2.4 us (3%)
    pallas_call x1, Pallas kernels, body(): pl.pallas_call(kernel, out_shape=(jax.ShapeDtypeStruct((4, 128), f32), ja...  85.1 us
    unnamed x10, local copies, waits for them, and re-layouts  4.12 us

profile of v1, /device:TPU:1, one launch (start us, length us, event | category | flops | bytes accessed | tf_op | source)
XLA Modules:
  0.0 91.6 jit_solution(13430541446293523563)
XLA Ops:
  0.6 0.0 copy-start.3
  0.6 0.7 copy-done.3
  1.3 0.0 copy-start
  1.3 0.8 copy-done
  2.1 0.0 copy-start.1
  2.1 0.8 copy-done.1
  2.9 0.0 copy-start.2
  2.9 0.7 copy-done.2
  3.6 85.1 %sinkhorn.1 = (f32[4,128]{1,0:T(4,128)S(1)}, f32[24,128]{1,0:T(8,128)S(1)}, f32[1,1]{1,0:T(1,128)}) custom-call(bf16[32,512]{1,0:T(8,128)(2,1)S(1)} %bitcast.8, bf16[8,3072]{1,0:T(8,128)(2,1)S(1)} %bitcast.7, f32[4,128]{1,0:T(4,128)S(1)} %bitcast.11, f32[24,128]{1,0:T(8,128)S(1)} %bitcast.9), custom_call_target="tpu_custom_call" | custom-call | tf_op jit(solution)/shard_map/sinkhorn/pallas_call | solution.py:240
  88.7 0.6 copy.10
  89.2 0.6 copy.11
Async XLA Ops:
  0.6 0.7 copy-start.3
  1.3 0.8 copy-start
  2.1 0.8 copy-start.1
  2.9 0.7 copy-start.2

commit v2 on v1

--- a/solution.py
+++ b/solution.py
@@ -17,6 +17,8 @@
 MESH = pl.DeviceIdType.MESH
 ROWS, COLS = 1024, 1536
 KT = COLS // 128
+CHUNKS = 2
+CHUNK = COLS // CHUNKS
 
 
 def coords():
@@ -67,8 +69,8 @@
 
 def kernel(
     xt, yt, a, b, f_out, g_out, loss_out,
-    XT, Y8, YM, S, VB, UB, ALL_A, ALL_B, LA, LB, XSQ, YSQ, GM, GS, FX, GX, FL, GL, GH,
-    ysem, xsem, asem, bsem, csem, local, fs, fr, gs, gr, ends,
+    XT, XR, Y8, YM, S, VB, UB, ALL_A, ALL_B, LA, LB, XSQ, YSQ, GM, GS, FX, GX, FL, GL, GH,
+    hsem, ysem, xsem, asem, bsem, csem, local, fs, fr, gs, gr, ends,
 ):
     co = coords()
     row, col = device(co)
@@ -77,7 +79,8 @@
     zc = co["z"] * 2 + co["c"]
     xy_peers = [at_offset(co, o) for o in offsets(["y", "xh", "xl"])]
     zc_peers = [at_offset(co, o) for o in offsets(["z", "c"])]
-    zx_peers = [at_offset(co, o) for o in offsets(["z", "xl"])]
+    z_peers = [at_offset(co, o) for o in offsets(["z"])]
+    across = at_offset(co, {"xl": 1})
     row_peers = [at_offset(co, o) for o in offsets(["z", "xl", "c"])]
     col_peers = [at_offset(co, o) for o in offsets(["y", "xh"])]
     barrier_peers = row_peers + [at_offset(co, o) for o in offsets(["y", "xh", "xl"]) if o.get("y", 0) or o.get("xh", 0)]
@@ -87,28 +90,38 @@
     for t in barrier_peers:
         pl.semaphore_signal(barrier, inc=1, device_id=device(t), device_id_type=MESH)
 
-    own_x = pltpu.make_async_copy(xt, XT.at[co["xl"] * 8 + col], local.at[0])
-    own_x.start()
-    half = pl.ds(pl.multiple_of(co["xl"] * COLS, 128), COLS)
-    own_y = pltpu.make_async_copy(yt.at[:, half], Y8.at[co["c"], zx], local.at[1])
-    own_y.start()
-    ALL_A[row] = a[...]
-    ALL_B[col] = b[...]
+    def cut(xl, n):
+        return yt.at[:, pl.ds(pl.multiple_of(xl * COLS + n * CHUNK, 128), CHUNK)]
+
+    own = [
+        pltpu.make_async_copy(a, ALL_A.at[row], local.at[0]),
+        pltpu.make_async_copy(b, ALL_B.at[col], local.at[1]),
+        pltpu.make_async_copy(xt, XT.at[co["xl"] * 8 + col], local.at[2]),
+    ] + [pltpu.make_async_copy(cut(co["xl"], n), Y8.at[n, co["c"], zx], local.at[3 + n]) for n in range(CHUNKS)]
+    for copy in own:
+        copy.start()
     pl.semaphore_wait(barrier, len(barrier_peers))
 
-    for ty, tx in zip(zx_peers, xy_peers):
-        part = pl.ds(pl.multiple_of(ty["xl"] * COLS, 128), COLS)
-        send(yt.at[:, part], Y8.at[co["c"], zx], ysem.at[0], ysem.at[1], ty)
-        send(xt, XT.at[co["xl"] * 8 + col], xsem.at[0], xsem.at[1], tx)
+    for n in range(CHUNKS):
+        here = Y8.at[n, co["c"], zx]
+        send(cut(across["xl"], n), here, hsem.at[0], hsem.at[1 + n], across)
+    for n in range(CHUNKS):
+        for t in z_peers:
+            send(cut(co["xl"], n), Y8.at[n, co["c"], zx], ysem.at[0], ysem.at[1 + n], t)
+    for t in xy_peers:
+        send(xt, XT.at[co["xl"] * 8 + col], xsem.at[0], xsem.at[1], t)
+    for copy in own:
+        copy.wait()
     for t in row_peers:
         send(ALL_A.at[row], ALL_A.at[row], asem.at[0], asem.at[1], t)
     for t in col_peers:
         send(ALL_B.at[col], ALL_B.at[col], bsem.at[0], bsem.at[1], t)
 
-    own_x.wait()
-    own_y.wait()
-    drain(Y8.at[0, pl.ds(0, 15)], ysem.at[1])
-    send(Y8.at[co["c"]], Y8.at[co["c"]], csem.at[0], csem.at[1], sibling)
+    for n in range(CHUNKS):
+        landed = Y8.at[n, co["c"], co["z"] * 2 + across["xl"]]
+        drain(landed, hsem.at[1 + n])
+        for t in z_peers:
+            send(landed, landed, ysem.at[0], ysem.at[1 + n], t)
 
     drain(ALL_A.at[pl.ds(0, 31)], asem.at[1])
     drain(ALL_B.at[pl.ds(0, 7)], bsem.at[1])
@@ -118,29 +131,42 @@
     LA[...] = mine * LOG2E - log_a_norm
     whole_b = ALL_B[...].reshape(192, 128) * LOG2E
     log_b_norm = full_lse(whole_b)
-    b_all = b[...]
+    b_all = ALL_B[col]
     LB[...] = jnp.where(co["xl"] == 0, b_all[:KT], b_all[KT:]) * LOG2E - log_b_norm
     drain(XT.at[pl.ds(0, 15)], xsem.at[1])
     for p in range(8):
-        x = XT[p // 4 * 8 : p // 4 * 8 + 8, :, pl.ds((p % 4) * 128, 128)].astype(jnp.float32).reshape(F, 128)
+        x = XT[p // 4 * 8 : p // 4 * 8 + 8, :, pl.ds((p % 4) * 128, 128)].reshape(F, 128)
+        XR[p * 128 : (p + 1) * 128, :] = x.T
+        x = x.astype(jnp.float32)
         XSQ[p : p + 1, :] = jnp.sum(x * x, axis=0, keepdims=True)
-    drain(Y8.at[0], csem.at[1])
-
-    def assemble(q, total):
-        y = jnp.concatenate([Y8[0, q].astype(jnp.float32), Y8[1, q].astype(jnp.float32)], axis=0)
-        YM[pl.ds(pl.multiple_of(q * 16, 16), 16), :] = y.astype(jnp.bfloat16)
-        return total + y * y
-
-    total = lax.fori_loop(0, 16, assemble, jnp.zeros((16, COLS), jnp.float32))
-    total = jnp.sum(total, axis=0, keepdims=True)
-    for k in range(KT):
-        YSQ[k : k + 1, :] = total[:, k * 128 : (k + 1) * 128]
 
     scale = 2.0 / F / EPS * LOG2E
-    for p in range(8):
-        x = XT[p // 4 * 8 : p // 4 * 8 + 8, :, pl.ds((p % 4) * 128, 128)].reshape(F, 128)
-        inner = lax.dot_general(x, YM[...], (((0,), (0,)), ((), ())), preferred_element_type=jnp.float32)
-        S[pl.ds(p * 128, 128), :] = inner * scale
+
+    def multiply(n):
+        drain(Y8.at[n, 0], csem.at[1 + n])
+        total = jnp.zeros((16, CHUNK), jnp.float32)
+        for q in range(16):
+            y = jnp.concatenate([Y8[n, 0, q].astype(jnp.float32), Y8[n, 1, q].astype(jnp.float32)], axis=0)
+            YM[q * 16 : (q + 1) * 16, n * CHUNK : (n + 1) * CHUNK] = y.astype(jnp.bfloat16)
+            total = total + y * y
+        total = jnp.sum(total, axis=0, keepdims=True)
+        for k in range(CHUNK // 128):
+            at = n * (CHUNK // 128) + k
+            YSQ[at : at + 1, :] = total[:, k * 128 : (k + 1) * 128]
+        for p in range(8):
+            inner = jnp.dot(
+                XR[p * 128 : (p + 1) * 128, :],
+                YM[:, n * CHUNK : (n + 1) * CHUNK],
+                preferred_element_type=jnp.float32,
+            )
+            S[p * 128 : (p + 1) * 128, n * CHUNK : (n + 1) * CHUNK] = inner * scale
+
+    for n in range(CHUNKS):
+        drain(Y8.at[n, 0, pl.ds(0, 14)], ysem.at[1 + n])
+        send(Y8.at[n, co["c"]], Y8.at[n, co["c"]], csem.at[0], csem.at[1 + n], sibling)
+        if n:
+            multiply(n - 1)
+    multiply(CHUNKS - 1)
 
     def set_v(v):
         for k in range(KT):
@@ -170,7 +196,7 @@
             FX[t, xy, pl.ds(p, 1), :] = top + jnp.log2(mass)
             return 0
 
-        lax.fori_loop(0, 8, row_block, 0)
+        lax.fori_loop(0, 8, row_block, 0, unroll=8)
         exchange(FX.at[t], xy, xy_peers, fs.at[t], fr.at[t])
         u = LA[...] - lse(FX[t])
         for p in range(8):
@@ -178,11 +204,11 @@
 
         def col_block(i, carry):
             peaks, masses = carry
-            us = [UB[pl.ds(pl.multiple_of(i * 64 + r * 8, 8), 8), :] for r in range(8)]
+            us = [UB[pl.ds(pl.multiple_of(i * 128 + r * 8, 8), 8), :] for r in range(16)]
             new_peaks, new_masses = [], []
             for k in range(KT):
                 tiles = [
-                    S[pl.ds(pl.multiple_of(i * 64 + r * 8, 8), 8), k * 128 : (k + 1) * 128] + us[r] for r in range(8)
+                    S[pl.ds(pl.multiple_of(i * 128 + r * 8, 8), 8), k * 128 : (k + 1) * 128] + us[r] for r in range(16)
                 ]
                 peak = functools.reduce(jnp.maximum, tiles + [peaks[k]])
                 mass = functools.reduce(jnp.add, [jnp.exp2(s - peak) for s in tiles])
@@ -191,7 +217,7 @@
             return new_peaks, new_masses
 
         start = [jnp.full((8, 128), -jnp.inf, jnp.float32)] * KT, [jnp.zeros((8, 128), jnp.float32)] * KT
-        peaks, masses = lax.fori_loop(0, ROWS // 64, col_block, start)
+        peaks, masses = lax.fori_loop(0, ROWS // 128, col_block, start, unroll=8)
         for k in range(KT):
             top = jnp.max(peaks[k], axis=0, keepdims=True)
             GM[k : k + 1, :] = top
@@ -210,7 +236,7 @@
     GH[co["xl"]] = g
     for t in xy_peers:
         send(GL.at[xy], GL.at[xy], ends.at[0], ends.at[1], t)
-    send(GH.at[co["xl"]], GH.at[co["xl"]], ends.at[2], ends.at[3], at_offset(co, {"xl": 1}))
+    send(GH.at[co["xl"]], GH.at[co["xl"]], ends.at[2], ends.at[3], across)
     for t in zc_peers:
         send(FL.at[zc], FL.at[zc], ends.at[4], ends.at[5], t)
     f_out[...] = jnp.where(co["xl"] == 0, f[:4], f[4:])
@@ -225,17 +251,18 @@
     drain(GL.at[pl.ds(0, 15)], ends.at[0])
     drain(GH.at[0], ends.at[2])
     drain(FL.at[pl.ds(0, 15)], ends.at[4])
-    drain(Y8.at[0, pl.ds(0, 15)], ysem.at[0])
+    drain(Y8.at[:, 0, 0], hsem.at[0])
+    drain(Y8.at[:, 0, pl.ds(0, 14)], ysem.at[0])
     drain(XT.at[pl.ds(0, 15)], xsem.at[0])
     drain(ALL_A.at[pl.ds(0, 31)], asem.at[0])
     drain(ALL_B.at[pl.ds(0, 7)], bsem.at[0])
-    drain(Y8.at[0], csem.at[0])
+    drain(Y8.at[:, 0], csem.at[0])
 
 
 def body(x_feat, y_feat, a_logits, b_logits):
     f32, bf16 = jnp.float32, jnp.bfloat16
     vmem = pl.BlockSpec(memory_space=pltpu.VMEM)
-    hbm = pl.BlockSpec(memory_space=pl.ANY)
+    hbm = pl.BlockSpec(memory_space=pltpu.HBM)
     dma = pltpu.SemaphoreType.DMA
     f, g, loss = pl.pallas_call(
         kernel,
@@ -244,11 +271,12 @@
             jax.ShapeDtypeStruct((24, 128), f32),
             jax.ShapeDtypeStruct((1, 1), f32),
         ),
-        in_specs=[hbm, hbm, vmem, vmem],
+        in_specs=[hbm, hbm, hbm, hbm],
         out_specs=(vmem, vmem, vmem),
         scratch_shapes=[
             pltpu.VMEM((16, 32, 512), bf16),
-            pltpu.VMEM((2, 16, 8, COLS), bf16),
+            pltpu.VMEM((ROWS, F), bf16),
+            pltpu.VMEM((CHUNKS, 2, 16, 8, CHUNK), bf16),
             pltpu.VMEM((F, COLS), bf16),
             pltpu.VMEM((ROWS, COLS), f32),
             pltpu.VMEM((8, COLS), f32),
@@ -266,12 +294,13 @@
             pltpu.VMEM((16, 8, 128), f32),
             pltpu.VMEM((16, KT, 128), f32),
             pltpu.VMEM((2, KT, 128), f32),
+            dma((1 + CHUNKS,)),
+            dma((1 + CHUNKS,)),
             dma((2,)),
             dma((2,)),
             dma((2,)),
-            dma((2,)),
-            dma((2,)),
-            dma((2,)),
+            dma((1 + CHUNKS,)),
+            dma((3 + CHUNKS,)),
             dma((ITERS,)),
             dma((ITERS,)),
             dma((ITERS,)),
@@ -279,7 +308,7 @@
             dma((6,)),
         ],
         compiler_params=pltpu.CompilerParams(
-            collective_id=0, has_side_effects=True, vmem_limit_bytes=40 * 1024 * 1024
+            collective_id=0, has_side_effects=True, vmem_limit_bytes=63 * 1024 * 1024
         ),
         name="sinkhorn",
     )(x_feat.T, y_feat.T, a_logits.reshape(4, 128), b_logits.reshape(24, 128))

time: 91.9 us -> 83.4 us (0.908)
  Pallas kernels: 85.1 us -> 79 us
  local copies, waits for them, and re-layouts: 4.12 us -> 1.86 us
    pallas_call x1, Pallas kernels: 85.1 us -> 79 us  [body(): pl.pallas_call(kernel, out_shape=(jax.ShapeDtypeStruct((4, 128), f32), ja...]
    unnamed x10 -> x4, local copies, waits for them, and re-layouts: 4.12 us -> 1.86 us
where the time goes in v2:
time: 83.4 us; the launch traced here: 83.3 us
  Pallas kernels  79 us (95%)
  between operations  2.39 us (3%)
  local copies, waits for them, and re-layouts  1.86 us (2%)
    pallas_call x1, Pallas kernels, body(): pl.pallas_call(kernel, out_shape=(jax.ShapeDtypeStruct((4, 128), f32), ja...  79 us
    unnamed x4, local copies, waits for them, and re-layouts  1.86 us

profile of v2, /device:TPU:1, one launch (start us, length us, event | category | flops | bytes accessed | tf_op | source)
XLA Modules:
  0.0 83.3 jit_solution(8712011656514340751)
XLA Ops:
  0.6 79.0 %sinkhorn.1 = (f32[4,128]{1,0:T(4,128)}, f32[24,128]{1,0:T(8,128)}, f32[1,1]{1,0:T(1,128)}) custom-call(bf16[32,512]{1,0:T(8,128)(2,1)} %bitcast.8, bf16[8,3072]{1,0:T(8,128)(2,1)} %bitcast.7, f32[4,128]{1,0:T(4,128)} %bitcast.11, f32[24,128]{1,0:T(8,128)} %bitcast.9), custom_call_target="tpu_custom_call" | custom-call | tf_op jit(solution)/shard_map/sinkhorn/pallas_call | solution.py:267
  79.7 0.0 copy-start
  79.7 1.3 %copy.10 = f32[512]{0:T(512)} copy(f32[512]{0:T(512)} %bitcast.12) | data formatting | bytes 4096
  80.9 0.0 copy-done
  80.9 0.6 copy.11
Async XLA Ops:
  79.7 1.3 %copy-start = (f32[24,128]{1,0:T(8,128)S(1)}, f32[24,128]{1,0:T(8,128)}, u32[]{:S(2)}) copy-start(f32[24,128]{1,0:T(8,128)} %get-tuple-element.7) | copy-start | bytes 36868

commit v3 on v2

v3 whole, which is shorter than its diff:
```python
import functools
import math

import jax
import jax.numpy as jnp
from jax import lax
from jax.experimental import pallas as pl
from jax.experimental.pallas import tpu as pltpu
from jax.sharding import PartitionSpec as P

ITERS = 4
EPS = 0.05
LN2 = math.log(2.0)
LOG2E = 1.0 / LN2
F = 256
SIZE = {"z": 8, "xl": 2, "c": 2, "y": 4, "xh": 2}
MESH = pl.DeviceIdType.MESH
ROWS, COLS = 2048, 1536
PARTS = 4
KT = COLS // 128
CHUNKS = 3
CHUNK = COLS // CHUNKS
GROUP = 4


def coords():
    r = lax.axis_index("row")
    k = lax.axis_index("col")
    return {"z": r // 4, "xl": lax.rem(r // 2, 2), "c": lax.rem(r, 2), "y": k // 2, "xh": lax.rem(k, 2)}


def device(o):
    return ((o["z"] * 2 + o["xl"]) * 2 + o["c"], o["y"] * 2 + o["xh"])


def hops(o):
    z, y = o.get("z", 0), o.get("y", 0)
    return min(z, 8 - z) + min(y, 4 - y) + 2 * o.get("xh", 0) + o.get("xl", 0)


def offsets(names):
    out = [{}]
    for n in names:
        out = [{**o, n: d} for o in out for d in range(SIZE[n])]
    return sorted([o for o in out if any(o.values())], key=lambda o: -hops(o))


def at_offset(co, o, c):
    return {n: (lax.rem(co[n] + o[n], SIZE[n]) if o.get(n, 0) else co[n]) for n in co} | {"c": c}


def send(src, dst, ssem, rsem, target):
    pltpu.make_async_remote_copy(
        src_ref=src, dst_ref=dst, send_sem=ssem, recv_sem=rsem, device_id=device(target), device_id_type=MESH
    ).start()


def drain(ref, sem):
    pltpu.make_async_copy(ref, ref, sem).wait()


def lse(x):
    peak = jnp.max(x, axis=0)
    return peak + jnp.log2(jnp.sum(jnp.exp2(x - peak[None]), axis=0))


def full_lse(x):
    peak = jnp.max(x, axis=(0, 1), keepdims=True)
    return peak + jnp.log2(jnp.sum(jnp.exp2(x - peak), axis=(0, 1), keepdims=True))


def kernel(
    xt, yt, a, b, f_out, g_out, loss_out,
    XT, XR, Y8, YM, S, VB, UB, AA, OWN_B, NA, NB, LA, LB, LBN, XSQ, YSQ, GM, GS, FX, GX, FL, GL, GH, FO, LO,
    hsem, ysem, xsem, asem, nsem, local, fs, fr, gs, gr, ends,
):
    co = coords()
    row, col = device(co)
    c = co["c"]
    xy = (co["xh"] * 2 + co["xl"]) * 4 + co["y"]
    zed = co["z"]
    xy_offsets = offsets(["y", "xh", "xl"])
    z_offsets = offsets(["z"])
    xy_peers = [at_offset(co, o, 1) for o in xy_offsets]
    z_peers = [at_offset(co, o, 1) for o in z_offsets]
    across = at_offset(co, {"xl": 1}, 1)
    sibling = at_offset(co, {}, 1 - c)
    worker = c == 1
    helper = c == 0

    barrier = pltpu.get_barrier_semaphore()

    def greet(t):
        pl.semaphore_signal(barrier, inc=1, device_id=device(t), device_id_type=MESH)

    @pl.when(worker)
    def _():
        for o in xy_offsets + z_offsets:
            greet(at_offset(co, o, 0))
            greet(at_offset(co, o, 1))
        greet(sibling)

    @pl.when(helper)
    def _():
        greet(sibling)

    def cut(xl, n):
        return yt.at[:, pl.ds(pl.multiple_of(xl * COLS + n * CHUNK, 128), CHUNK)]

    own = [
        pltpu.make_async_copy(xt, XT.at[row % 4 * 8 + col], local.at[0]),
        pltpu.make_async_copy(a, AA.at[row % 4], local.at[1]),
        pltpu.make_async_copy(b, OWN_B, local.at[2]),
    ] + [pltpu.make_async_copy(cut(co["xl"], n), Y8.at[n, row], local.at[3 + n]) for n in range(CHUNKS)]

    @pl.when(worker)
    def _():
        for copy in own:
            copy.start()

    pl.semaphore_wait(barrier, len(xy_offsets) + len(z_offsets) + 1)

    for n in range(CHUNKS):
        send(cut(across["xl"], n), Y8.at[n, row], hsem.at[0], hsem.at[1 + n], across)
    for n in range(CHUNKS):
        for t in z_peers:
            send(cut(co["xl"], n), Y8.at[n, row], ysem.at[0], ysem.at[1 + n], t)
    for t in xy_peers:
        send(xt, XT.at[row % 4 * 8 + col], xsem.at[0], xsem.at[1], t)
    send(a, AA.at[row % 4], asem.at[0], asem.at[1], across)

    @pl.when(helper)
    def _():
        for n in range(CHUNKS):
            send(cut(co["xl"], n), Y8.at[n, row], ysem.at[0], ysem.at[1 + n], sibling)
        send(xt, XT.at[row % 4 * 8 + col], xsem.at[0], xsem.at[1], sibling)
        send(a, AA.at[row % 4], asem.at[0], asem.at[1], sibling)
        drain(Y8.at[0, pl.ds(0, CHUNKS)], hsem.at[0])
        drain(Y8.at[0, pl.ds(0, CHUNKS * 8)], ysem.at[0])
        drain(XT.at[pl.ds(0, 16)], xsem.at[0])
        drain(AA.at[pl.ds(0, 2)], asem.at[0])
        drain(FO, ends.at[5])
        drain(GH, ends.at[7])
        drain(LO, ends.at[9])
        f_out[...] = FO[...]
        g_out[:KT] = GH[0]
        g_out[KT:] = GH[1]
        loss_out[...] = LO[0:1, 0:1]

    @pl.when(worker)
    def _():
        work(
            co, row, col, xy, zed, xy_peers, z_peers, across, sibling, own, f_out, g_out, loss_out,
            XT, XR, Y8, YM, S, VB, UB, AA, OWN_B, NA, NB, LA, LB, LBN, XSQ, YSQ, GM, GS, FX, GX, FL, GL, GH, FO, LO,
            hsem, ysem, xsem, asem, nsem, fs, fr, gs, gr, ends,
        )


def work(
    co, row, col, xy, zed, xy_peers, z_peers, across, sibling, own, f_out, g_out, loss_out,
    XT, XR, Y8, YM, S, VB, UB, AA, OWN_B, NA, NB, LA, LB, LBN, XSQ, YSQ, GM, GS, FX, GX, FL, GL, GH, FO, LO,
    hsem, ysem, xsem, asem, nsem, fs, fr, gs, gr, ends,
):
    other = co["z"] * 4 + across["xl"] * 2
    for n in range(CHUNKS):
        landed = Y8.at[n, pl.ds(other, 2)]
        drain(landed, hsem.at[1 + n])
        for t in z_peers:
            send(landed, landed, ysem.at[0], ysem.at[1 + n], t)

    for copy in own:
        copy.wait()
    own_b = jnp.where(co["xl"] == 0, OWN_B[:KT], OWN_B[KT:]) * LOG2E
    LB[...] = own_b
    NB[xy] = jnp.broadcast_to(full_lse(own_b), (1, 128))
    for t in xy_peers:
        send(NB.at[xy], NB.at[xy], nsem.at[0], nsem.at[1], t)
    drain(AA.at[pl.ds(0, 3)], asem.at[1])
    whole_a = AA[...].reshape(16, 128) * LOG2E
    LA[...] = whole_a
    NA[zed] = jnp.broadcast_to(full_lse(whole_a), (1, 128))
    for t in z_peers:
        send(NA.at[zed], NA.at[zed], nsem.at[2], nsem.at[3], t)

    drain(XT.at[pl.ds(0, 31)], xsem.at[1])
    for p in range(16):
        x = XT[p // 4 * 8 : p // 4 * 8 + 8, :, pl.ds((p % 4) * 128, 128)].reshape(F, 128)
        XR[p * 128 : (p + 1) * 128, :] = x.T
        x = x.astype(jnp.float32)
        XSQ[p : p + 1, :] = jnp.sum(x * x, axis=0, keepdims=True)

    def set_v(v, first, count):
        for k in range(count):
            at = first + k
            VB[:, at * 128 : (at + 1) * 128] = jnp.broadcast_to(v[k : k + 1, :], (8, 128))

    scale = 2.0 / F / EPS * LOG2E
    tiles_in = CHUNK // 128
    for n in range(CHUNKS):
        drain(Y8.at[n, pl.ds(0, 29)], ysem.at[1 + n])
        span = slice(n * CHUNK, (n + 1) * CHUNK)
        total = jnp.zeros((16, CHUNK), jnp.float32)
        for q in range(16):
            y = jnp.concatenate(
                [Y8[n, 2 * q].astype(jnp.float32), Y8[n, 2 * q + 1].astype(jnp.float32)], axis=0
            )
            YM[q * 16 : (q + 1) * 16, span] = y.astype(jnp.bfloat16)
            total = total + y * y
        total = jnp.sum(total, axis=0, keepdims=True)
        for k in range(tiles_in):
            at = n * tiles_in + k
            YSQ[at : at + 1, :] = total[:, k * 128 : (k + 1) * 128]
        mine = slice(n * tiles_in, (n + 1) * tiles_in)
        set_v(LB[mine] - YSQ[mine] * (LOG2E / F / EPS), n * tiles_in, tiles_in)

        def multiply(p, _):
            at = pl.ds(pl.multiple_of(p * 128, 128), 128)
            inner = jnp.dot(XR[at, :], YM[:, span], preferred_element_type=jnp.float32)
            S[at, span] = inner * scale
            return 0

        lax.fori_loop(0, 16, multiply, 0, unroll=4)

    def f_pass(t):
        def part(h, _):
            for q in range(4):
                peaks, masses = [], []
                for r in range(16):
                    at = pl.ds(pl.multiple_of(h * 512 + q * 128 + r * 8, 8), 8)
                    tiles = [S[at, k * 128 : (k + 1) * 128] + VB[:, k * 128 : (k + 1) * 128] for k in range(KT)]
                    peak = functools.reduce(jnp.maximum, tiles)
                    peaks.append(peak)
                    masses.append(functools.reduce(jnp.add, [jnp.exp2(s - peak) for s in tiles]))
                peak = jnp.concatenate(peaks, axis=0).T
                mass = jnp.concatenate(masses, axis=0).T
                top = jnp.max(peak, axis=0, keepdims=True)
                mass = jnp.sum(mass * jnp.exp2(peak - top), axis=0, keepdims=True)
                FX[t, h, xy, q : q + 1, :] = top + jnp.log2(mass)
            for peer in xy_peers:
                send(FX.at[t, h, xy], FX.at[t, h, xy], fs.at[t], fr.at[t, h], peer)
            return 0

        lax.fori_loop(0, PARTS, part, 0)

    def g_pass(t):
        def part(h, _):
            drain(FX.at[t, h, pl.ds(0, 15)], fr.at[t, h])
            rows = pl.ds(pl.multiple_of(h * 4, 4), 4)
            u = LA[rows, :] - (lse(FX[t, h]) - jnp.where(t == 0, LBN[...], 0.0))
            for q in range(4):
                UB[q * 128 : (q + 1) * 128, :] = jnp.broadcast_to(u[q : q + 1, :], (128, 128)).T
            for k0 in range(0, KT, GROUP):
                span = slice(k0 * 128, (k0 + GROUP) * 128)
                peaks = [GM[:, k * 128 : (k + 1) * 128] for k in range(k0, k0 + GROUP)]
                masses = [GS[:, k * 128 : (k + 1) * 128] for k in range(k0, k0 + GROUP)]
                for q in range(4):
                    us = [UB[q * 128 + r * 8 : q * 128 + r * 8 + 8, :] for r in range(16)]
                    for k in range(GROUP):
                        lanes = slice((k0 + k) * 128, (k0 + k + 1) * 128)
                        tiles = [
                            S[pl.ds(pl.multiple_of(h * 512 + q * 128 + r * 8, 8), 8), lanes] + us[r]
                            for r in range(16)
                        ]
                        peak = functools.reduce(jnp.maximum, tiles + [peaks[k]])
                        mass = functools.reduce(jnp.add, [jnp.exp2(s - peak) for s in tiles])
                        masses[k] = mass + masses[k] * jnp.exp2(peaks[k] - peak)
                        peaks[k] = peak
                for k in range(GROUP):
                    lanes = slice((k0 + k) * 128, (k0 + k + 1) * 128)
                    GM[:, lanes] = peaks[k]
                    GS[:, lanes] = masses[k]
            return 0

        GM[...] = jnp.full(GM.shape, -jnp.inf, jnp.float32)
        GS[...] = jnp.zeros(GS.shape, jnp.float32)
        lax.fori_loop(0, PARTS, part, 0)
        for k in range(KT):
            lanes = slice(k * 128, (k + 1) * 128)
            peak = GM[:, lanes]
            top = jnp.max(peak, axis=0, keepdims=True)
            mass = jnp.sum(GS[:, lanes] * jnp.exp2(peak - top), axis=0, keepdims=True)
            GX[t, zed, k : k + 1, :] = top + jnp.log2(mass)
        for peer in z_peers:
            send(GX.at[t, zed], GX.at[t, zed], gs.at[t], gr.at[t], peer)
        drain(GX.at[t, pl.ds(0, 7)], gr.at[t])

    f_pass(0)
    drain(NB.at[pl.ds(0, 15)], nsem.at[1])
    drain(NA.at[pl.ds(0, 7)], nsem.at[3])
    log_b_norm = lse(NB[...])
    log_a_norm = lse(NA[...])
    LB[...] = LB[...] - log_b_norm
    LA[...] = LA[...] - log_a_norm
    LBN[...] = log_b_norm

    def iteration(t, _):
        g_pass(t)

        @pl.when(t < ITERS - 1)
        def _():
            set_v(LB[...] - lse(GX[t]), 0, KT)
            f_pass(t + 1)

        return 0

    lax.fori_loop(0, ITERS, iteration, 0)
    last = ITERS - 1
    g = YSQ[...] * (1.0 / F) - lse(GX[last]) * (EPS * LN2)
    GL[xy] = jnp.sum(jnp.exp2(LB[...]) * g, axis=0, keepdims=True)
    GH[co["xl"]] = g
    for t in xy_peers:
        send(GL.at[xy], GL.at[xy], ends.at[0], ends.at[1], t)
    send(GH.at[co["xl"]], GH.at[co["xl"]], ends.at[2], ends.at[3], across)
    lam = jnp.concatenate([lse(FX[last, h]) for h in range(PARTS)], axis=0)
    f = XSQ[...] * (1.0 / F) - lam * (EPS * LN2)
    FL[zed] = jnp.sum(jnp.exp2(LA[...]) * f, axis=0, keepdims=True)
    for t in z_peers:
        send(FL.at[zed], FL.at[zed], ends.at[10], ends.at[11], t)
    FO[...] = jnp.where(co["xl"] == 0, f[0:4], f[8:12])
    send(FO, FO, ends.at[4], ends.at[5], sibling)
    f_out[...] = jnp.where(co["xl"] == 0, f[4:8], f[12:16])
    drain(GH.at[0], ends.at[3])
    send(GH, GH, ends.at[6], ends.at[7], sibling)
    g_out[:KT] = GH[0]
    g_out[KT:] = GH[1]
    drain(FL.at[pl.ds(0, 7)], ends.at[11])
    drain(GL.at[pl.ds(0, 15)], ends.at[1])
    loss = jnp.sum(jnp.sum(FL[...], axis=0), axis=(0, 1), keepdims=True) + jnp.sum(
        jnp.sum(GL[...], axis=0), axis=(0, 1), keepdims=True
    )
    LO[...] = jnp.broadcast_to(loss, (1, 128))
    send(LO, LO, ends.at[8], ends.at[9], sibling)
    loss_out[...] = loss

    drain(GL.at[pl.ds(0, 15)], ends.at[0])
    drain(GH.at[0], ends.at[2])
    drain(FO, ends.at[4])
    drain(GH, ends.at[6])
    drain(LO, ends.at[8])
    drain(FL.at[pl.ds(0, 7)], ends.at[10])
    for t in range(ITERS):
        drain(FX.at[t, :, pl.ds(0, 15)], fs.at[t])
        drain(GX.at[t, pl.ds(0, 7)], gs.at[t])
    drain(NB.at[pl.ds(0, 15)], nsem.at[0])
    drain(NA.at[pl.ds(0, 7)], nsem.at[2])
    drain(Y8.at[0, pl.ds(0, CHUNKS)], hsem.at[0])
    drain(Y8.at[:, pl.ds(0, 21)], ysem.at[0])
    drain(XT.at[pl.ds(0, 15)], xsem.at[0])
    drain(AA.at[0], asem.at[0])


def body(x_feat, y_feat, a_logits, b_logits):
    f32, bf16 = jnp.float32, jnp.bfloat16
    vmem = pl.BlockSpec(memory_space=pltpu.VMEM)
    hbm = pl.BlockSpec(memory_space=pltpu.HBM)
    dma = pltpu.SemaphoreType.DMA
    f, g, loss = pl.pallas_call(
        kernel,
        out_shape=(
            jax.ShapeDtypeStruct((4, 128), f32),
            jax.ShapeDtypeStruct((24, 128), f32),
            jax.ShapeDtypeStruct((1, 1), f32),
        ),
        in_specs=[hbm, hbm, hbm, hbm],
        out_specs=(vmem, vmem, vmem),
        scratch_shapes=[
            pltpu.VMEM((32, 32, 512), bf16),
            pltpu.VMEM((ROWS, F), bf16),
            pltpu.VMEM((CHUNKS, 32, 8, CHUNK), bf16),
            pltpu.VMEM((F, COLS), bf16),
            pltpu.VMEM((ROWS, COLS), f32),
            pltpu.VMEM((8, COLS), f32),
            pltpu.VMEM((512, 128), f32),
            pltpu.VMEM((4, 4, 128), f32),
            pltpu.VMEM((24, 128), f32),
            pltpu.VMEM((8, 1, 128), f32),
            pltpu.VMEM((16, 1, 128), f32),
            pltpu.VMEM((16, 128), f32),
            pltpu.VMEM((KT, 128), f32),
            pltpu.VMEM((1, 128), f32),
            pltpu.VMEM((16, 128), f32),
            pltpu.VMEM((KT, 128), f32),
            pltpu.VMEM((8, COLS), f32),
            pltpu.VMEM((8, COLS), f32),
            pltpu.VMEM((ITERS, PARTS, 16, 4, 128), f32),
            pltpu.VMEM((ITERS, 8, KT, 128), f32),
            pltpu.VMEM((8, 1, 128), f32),
            pltpu.VMEM((16, 1, 128), f32),
            pltpu.VMEM((2, KT, 128), f32),
            pltpu.VMEM((4, 128), f32),
            pltpu.VMEM((1, 128), f32),
            dma((1 + CHUNKS,)),
            dma((1 + CHUNKS,)),
            dma((2,)),
            dma((2,)),
            dma((4,)),
            dma((3 + CHUNKS,)),
            dma((ITERS,)),
            dma((ITERS, PARTS)),
            dma((ITERS,)),
            dma((ITERS,)),
            dma((12,)),
        ],
        compiler_params=pltpu.CompilerParams(
            collective_id=0, has_side_effects=True, vmem_limit_bytes=63 * 1024 * 1024
        ),
        name="sinkhorn",
    )(x_feat.T, y_feat.T, a_logits.reshape(4, 128), b_logits.reshape(24, 128))
    return f.reshape(512), g.reshape(3072), loss.reshape(())


def solution(mesh):
    in_specs = (P("row", "col"), P("col", "row"), P("row"), P("col"))
    out_specs = (P("row"), P("col"), P())
    return jax.shard_map(body, mesh=mesh, in_specs=in_specs, out_specs=out_specs, check_vma=False)
```

time: 83.4 us -> 80.6 us (0.966)
  Pallas kernels: 79 us -> 76.2 us
    pallas_call x1, Pallas kernels: 79 us -> 76.2 us  [body(): pl.pallas_call(kernel, out_shape=(jax.ShapeDtypeStruct((4, 128), f32), ja...]
where the time goes in v3:
time: 80.6 us; the launch traced here: 80.4 us
  Pallas kernels  76.2 us (95%)
  between operations  2.39 us (3%)
  local copies, waits for them, and re-layouts  1.86 us (2%)
    pallas_call x1, Pallas kernels, body(): pl.pallas_call(kernel, out_shape=(jax.ShapeDtypeStruct((4, 128), f32), ja...  76.2 us
    unnamed x4, local copies, waits for them, and re-layouts  1.86 us

profile of v3, /device:TPU:1, one launch (start us, length us, event | category | flops | bytes accessed | tf_op | source)
XLA Modules:
  0.0 80.4 jit_solution(15788942402992781902)
XLA Ops:
  0.6 76.2 %sinkhorn.1 = (f32[4,128]{1,0:T(4,128)}, f32[24,128]{1,0:T(8,128)}, f32[1,1]{1,0:T(1,128)}) custom-call(bf16[32,512]{1,0:T(8,128)(2,1)} %bitcast.8, bf16[8,3072]{1,0:T(8,128)(2,1)} %bitcast.7, f32[4,128]{1,0:T(4,128)} %bitcast.11, f32[24,128]{1,0:T(8,128)} %bitcast.9), custom_call_target="tpu_custom_call" | custom-call | tf_op jit(solution)/shard_map/sinkhorn/pallas_call | solution.py:357
  76.8 0.0 copy-start
  76.8 1.3 %copy.10 = f32[512]{0:T(512)} copy(f32[512]{0:T(512)} %bitcast.12) | data formatting | bytes 4096
  78.1 0.0 copy-done
  78.1 0.6 copy.11
Async XLA Ops:
  76.8 1.3 %copy-start = (f32[24,128]{1,0:T(8,128)S(1)}, f32[24,128]{1,0:T(8,128)}, u32[]{:S(2)}) copy-start(f32[24,128]{1,0:T(8,128)} %get-tuple-element.7) | copy-start | bytes 36868

commit v4 on v3

--- a/solution.py
+++ b/solution.py
@@ -64,14 +64,20 @@
     return peak + jnp.log2(jnp.sum(jnp.exp2(x - peak[None]), axis=0))
 
 
+def tree(op, xs):
+    while len(xs) > 1:
+        xs = [op(xs[i], xs[i + 1]) if i + 1 < len(xs) else xs[i] for i in range(0, len(xs), 2)]
+    return xs[0]
+
+
 def full_lse(x):
     peak = jnp.max(x, axis=(0, 1), keepdims=True)
     return peak + jnp.log2(jnp.sum(jnp.exp2(x - peak), axis=(0, 1), keepdims=True))
 
 
 def kernel(
-    xt, yt, a, b, f_out, g_out, loss_out,
-    XT, XR, Y8, YM, S, VB, UB, AA, OWN_B, NA, NB, LA, LB, LBN, XSQ, YSQ, GM, GS, FX, GX, FL, GL, GH, FO, LO,
+    fast, xt, yt, a, b, f_out, g_out, loss_out,
+    XT, XR, Y8, YM, S, VB, UB, ZB, AA, OWN_B, NA, NB, LA, LB, LBN, XSQ, YSQ, GM, GS, FX, GX, FL, GL, GH, FO, LO, FP, FM, LAM, BADR, BADC,
     hsem, ysem, xsem, asem, nsem, local, fs, fr, gs, gr, ends,
 ):
     co = coords()
@@ -150,15 +156,15 @@
     @pl.when(worker)
     def _():
         work(
-            co, row, col, xy, zed, xy_peers, z_peers, across, sibling, own, f_out, g_out, loss_out,
-            XT, XR, Y8, YM, S, VB, UB, AA, OWN_B, NA, NB, LA, LB, LBN, XSQ, YSQ, GM, GS, FX, GX, FL, GL, GH, FO, LO,
+            fast, co, row, col, xy, zed, xy_peers, z_peers, across, sibling, own, f_out, g_out, loss_out,
+            XT, XR, Y8, YM, S, VB, UB, ZB, AA, OWN_B, NA, NB, LA, LB, LBN, XSQ, YSQ, GM, GS, FX, GX, FL, GL, GH, FO, LO, FP, FM, LAM, BADR, BADC,
             hsem, ysem, xsem, asem, nsem, fs, fr, gs, gr, ends,
         )
 
 
 def work(
-    co, row, col, xy, zed, xy_peers, z_peers, across, sibling, own, f_out, g_out, loss_out,
-    XT, XR, Y8, YM, S, VB, UB, AA, OWN_B, NA, NB, LA, LB, LBN, XSQ, YSQ, GM, GS, FX, GX, FL, GL, GH, FO, LO,
+    fast, co, row, col, xy, zed, xy_peers, z_peers, across, sibling, own, f_out, g_out, loss_out,
+    XT, XR, Y8, YM, S, VB, UB, ZB, AA, OWN_B, NA, NB, LA, LB, LBN, XSQ, YSQ, GM, GS, FX, GX, FL, GL, GH, FO, LO, FP, FM, LAM, BADR, BADC,
     hsem, ysem, xsem, asem, nsem, fs, fr, gs, gr, ends,
 ):
     other = co["z"] * 4 + across["xl"] * 2
@@ -193,6 +199,16 @@
         for k in range(count):
             at = first + k
             VB[:, at * 128 : (at + 1) * 128] = jnp.broadcast_to(v[k : k + 1, :], (8, 128))
+
+    def over_lanes(peaks, masses):
+        peak = jnp.concatenate(peaks, axis=0).T
+        mass = jnp.concatenate(masses, axis=0).T
+        top = jnp.max(peak, axis=0, keepdims=True)
+        return top + jnp.log2(jnp.sum(mass * jnp.exp2(peak - top), axis=0, keepdims=True))
+
+    def send_rows(t, h):
+        for peer in xy_peers:
+            send(FX.at[t, h, xy], FX.at[t, h, xy], fs.at[t], fr.at[t, h], peer)
 
     scale = 2.0 / F / EPS * LOG2E
     tiles_in = CHUNK // 128
@@ -221,6 +237,36 @@
 
         lax.fori_loop(0, 16, multiply, 0, unroll=4)
 
+        def first_rows(h, _):
+            for q in range(4):
+                peaks, masses = [], []
+                for r in range(16):
+                    at = pl.ds(pl.multiple_of(h * 512 + q * 128 + r * 8, 8), 8)
+                    tiles = [
+                        S[at, k * 128 : (k + 1) * 128] + VB[:, k * 128 : (k + 1) * 128]
+                        for k in range(n * tiles_in, (n + 1) * tiles_in)
+                    ]
+                    if n:
+                        before = FP[at, :]
+                        peak = tree(jnp.maximum, tiles + [before])
+                        mass = [jnp.exp2(s - peak) for s in tiles] + [FM[at, :] * jnp.exp2(before - peak)]
+                    else:
+                        peak = tree(jnp.maximum, tiles)
+                        mass = [jnp.exp2(s - peak) for s in tiles]
+                    mass = tree(jnp.add, mass)
+                    if n < CHUNKS - 1:
+                        FP[at, :] = peak
+                        FM[at, :] = mass
+                    peaks.append(peak)
+                    masses.append(mass)
+                if n == CHUNKS - 1:
+                    FX[0, h, xy, q : q + 1, :] = over_lanes(peaks, masses)
+            if n == CHUNKS - 1:
+                send_rows(0, h)
+            return 0
+
+        lax.fori_loop(0, PARTS, first_rows, 0)
+
     def f_pass(t):
         def part(h, _):
             for q in range(4):
@@ -231,16 +277,16 @@
                     peak = functools.reduce(jnp.maximum, tiles)
                     peaks.append(peak)
                     masses.append(functools.reduce(jnp.add, [jnp.exp2(s - peak) for s in tiles]))
-                peak = jnp.concatenate(peaks, axis=0).T
-                mass = jnp.concatenate(masses, axis=0).T
-                top = jnp.max(peak, axis=0, keepdims=True)
-                mass = jnp.sum(mass * jnp.exp2(peak - top), axis=0, keepdims=True)
-                FX[t, h, xy, q : q + 1, :] = top + jnp.log2(mass)
-            for peer in xy_peers:
-                send(FX.at[t, h, xy], FX.at[t, h, xy], fs.at[t], fr.at[t, h], peer)
+                FX[t, h, xy, q : q + 1, :] = over_lanes(peaks, masses)
+            send_rows(t, h)
             return 0
 
         lax.fori_loop(0, PARTS, part, 0)
+
+    def swap_columns(t):
+        for peer in z_peers:
+            send(GX.at[t, zed], GX.at[t, zed], gs.at[t], gr.at[t], peer)
+        drain(GX.at[t, pl.ds(0, 7)], gr.at[t])
 
     def g_pass(t):
         def part(h, _):
@@ -280,11 +326,75 @@
             top = jnp.max(peak, axis=0, keepdims=True)
             mass = jnp.sum(GS[:, lanes] * jnp.exp2(peak - top), axis=0, keepdims=True)
             GX[t, zed, k : k + 1, :] = top + jnp.log2(mass)
-        for peer in z_peers:
-            send(GX.at[t, zed], GX.at[t, zed], gs.at[t], gr.at[t], peer)
-        drain(GX.at[t, pl.ds(0, 7)], gr.at[t])
-
-    f_pass(0)
+        swap_columns(t)
+
+    def fast_rows(t):
+        def part(h, _):
+            for q in range(4):
+                sums = []
+                for r in range(16):
+                    at = pl.ds(pl.multiple_of(h * 512 + q * 128 + r * 8, 8), 8)
+                    sums.append(
+                        tree(
+                            jnp.add,
+                            [S[at, k * 128 : (k + 1) * 128] * VB[:, k * 128 : (k + 1) * 128] for k in range(KT)],
+                        )
+                    )
+                FX[t, h, xy, q : q + 1, :] = jnp.sum(jnp.concatenate(sums, axis=0).T, axis=0, keepdims=True)
+            send_rows(t, h)
+            return 0
+
+        lax.fori_loop(0, PARTS, part, 0)
+
+    def fast_columns(t, first):
+        def part(h, _):
+            drain(FX.at[t, h, pl.ds(0, 15)], fr.at[t, h])
+            rows = pl.ds(pl.multiple_of(h * 4, 4), 4)
+            mass_a = jnp.exp2(LA[rows, :])
+            if first:
+                lam = lse(FX[t, h])
+                LAM[rows, :] = lam - LBN[...]
+                zs = mass_a
+                for q in range(4):
+                    UB[q * 128 : (q + 1) * 128, :] = jnp.broadcast_to(lam[q : q + 1, :], (128, 128)).T
+            else:
+                total = jnp.sum(FX[t, h], axis=0)
+                zs = mass_a / total
+                good = jnp.logical_and(total >= 2.0**-35, zs <= 2.0**20)
+                BADR[...] = jnp.maximum(BADR[...], jnp.where(good, 0.0, 1.0))
+            for q in range(4):
+                ZB[q * 128 : (q + 1) * 128, :] = jnp.broadcast_to(zs[q : q + 1, :], (128, 128)).T
+            for k0 in range(0, KT, GROUP):
+                sums = [GS[:, k * 128 : (k + 1) * 128] for k in range(k0, k0 + GROUP)]
+                for q in range(4):
+                    at = [q * 128 + r * 8 for r in range(16)]
+                    z = [ZB[i : i + 8, :] for i in at]
+                    for k in range(GROUP):
+                        lanes = slice((k0 + k) * 128, (k0 + k + 1) * 128)
+                        terms = []
+                        for r in range(16):
+                            here = pl.ds(pl.multiple_of(h * 512 + at[r], 8), 8)
+                            p = S[here, lanes]
+                            if first:
+                                p = jnp.exp2(p + VB[:, lanes] - UB[at[r] : at[r] + 8, :])
+                                S[here, lanes] = p
+                            terms.append(p * z[r])
+                        sums[k] = sums[k] + tree(jnp.add, terms)
+                for k in range(GROUP):
+                    GS[:, (k0 + k) * 128 : (k0 + k + 1) * 128] = sums[k]
+            return 0
+
+        GS[...] = jnp.zeros(GS.shape, jnp.float32)
+        lax.fori_loop(0, PARTS, part, 0)
+        for k in range(KT):
+            GX[t, zed, k : k + 1, :] = jnp.sum(GS[:, k * 128 : (k + 1) * 128], axis=0, keepdims=True)
+        swap_columns(t)
+        total = jnp.sum(GX[t], axis=0)
+        w = jnp.exp2(LB[...]) / total
+        good = jnp.logical_and(total >= 2.0**-65, w <= 2.0**45)
+        BADC[...] = jnp.maximum(BADC[...], jnp.where(good, 0.0, 1.0))
+        return w
+
     drain(NB.at[pl.ds(0, 15)], nsem.at[1])
     drain(NA.at[pl.ds(0, 7)], nsem.at[3])
     log_b_norm = lse(NB[...])
@@ -292,28 +402,52 @@
     LB[...] = LB[...] - log_b_norm
     LA[...] = LA[...] - log_a_norm
     LBN[...] = log_b_norm
-
-    def iteration(t, _):
-        g_pass(t)
-
-        @pl.when(t < ITERS - 1)
-        def _():
-            set_v(LB[...] - lse(GX[t]), 0, KT)
-            f_pass(t + 1)
-
-        return 0
-
-    lax.fori_loop(0, ITERS, iteration, 0)
+    BADR[...] = jnp.zeros(BADR.shape, jnp.float32)
+    BADC[...] = jnp.zeros(BADC.shape, jnp.float32)
     last = ITERS - 1
-    g = YSQ[...] * (1.0 / F) - lse(GX[last]) * (EPS * LN2)
-    GL[xy] = jnp.sum(jnp.exp2(LB[...]) * g, axis=0, keepdims=True)
+
+    if fast:
+        set_v(fast_columns(0, True), 0, KT)
+        fast_rows(1)
+
+        def iteration(t, _):
+            w = fast_columns(t, False)
+
+            @pl.when(t < last)
+            def _():
+                set_v(w, 0, KT)
+                fast_rows(t + 1)
+
+            return 0
+
+        lax.fori_loop(1, ITERS, iteration, 0)
+        g = (LB[...] - jnp.log2(jnp.sum(GX[last], axis=0))) * (EPS * LN2)
+        lam = jnp.concatenate([jnp.sum(FX[last, h], axis=0) for h in range(PARTS)], axis=0)
+        lam = LAM[...] + jnp.log2(lam)
+    else:
+
+        def iteration(t, _):
+            g_pass(t)
+
+            @pl.when(t < last)
+            def _():
+                set_v(LB[...] - lse(GX[t]), 0, KT)
+                f_pass(t + 1)
+
+            return 0
+
+        lax.fori_loop(0, ITERS, iteration, 0)
+        g = YSQ[...] * (1.0 / F) - lse(GX[last]) * (EPS * LN2)
+        lam = jnp.concatenate([lse(FX[last, h]) for h in range(PARTS)], axis=0)
+    f = XSQ[...] * (1.0 / F) - lam * (EPS * LN2)
+
+    bad = jnp.maximum(jnp.max(BADR[...], axis=0, keepdims=True), jnp.max(BADC[...], axis=0, keepdims=True)) > 0.0
+    GL[xy] = jnp.where(bad, jnp.nan, jnp.sum(jnp.exp2(LB[...]) * g, axis=0, keepdims=True))
     GH[co["xl"]] = g
     for t in xy_peers:
         send(GL.at[xy], GL.at[xy], ends.at[0], ends.at[1], t)
     send(GH.at[co["xl"]], GH.at[co["xl"]], ends.at[2], ends.at[3], across)
-    lam = jnp.concatenate([lse(FX[last, h]) for h in range(PARTS)], axis=0)
-    f = XSQ[...] * (1.0 / F) - lam * (EPS * LN2)
-    FL[zed] = jnp.sum(jnp.exp2(LA[...]) * f, axis=0, keepdims=True)
+    FL[zed] = jnp.where(bad, jnp.nan, jnp.sum(jnp.exp2(LA[...]) * f, axis=0, keepdims=True))
     for t in z_peers:
         send(FL.at[zed], FL.at[zed], ends.at[10], ends.at[11], t)
     FO[...] = jnp.where(co["xl"] == 0, f[0:4], f[8:12])
@@ -349,13 +483,13 @@
     drain(AA.at[0], asem.at[0])
 
 
-def body(x_feat, y_feat, a_logits, b_logits):
+def whole(fast, x_feat, y_feat, a_logits, b_logits):
     f32, bf16 = jnp.float32, jnp.bfloat16
     vmem = pl.BlockSpec(memory_space=pltpu.VMEM)
     hbm = pl.BlockSpec(memory_space=pltpu.HBM)
     dma = pltpu.SemaphoreType.DMA
     f, g, loss = pl.pallas_call(
-        kernel,
+        functools.partial(kernel, fast),
         out_shape=(
             jax.ShapeDtypeStruct((4, 128), f32),
             jax.ShapeDtypeStruct((24, 128), f32),
@@ -370,6 +504,7 @@
             pltpu.VMEM((F, COLS), bf16),
             pltpu.VMEM((ROWS, COLS), f32),
             pltpu.VMEM((8, COLS), f32),
+            pltpu.VMEM((512, 128), f32),
             pltpu.VMEM((512, 128), f32),
             pltpu.VMEM((4, 4, 128), f32),
             pltpu.VMEM((24, 128), f32),
@@ -389,6 +524,11 @@
             pltpu.VMEM((2, KT, 128), f32),
             pltpu.VMEM((4, 128), f32),
             pltpu.VMEM((1, 128), f32),
+            pltpu.VMEM((ROWS, 128), f32),
+            pltpu.VMEM((ROWS, 128), f32),
+            pltpu.VMEM((16, 128), f32),
+            pltpu.VMEM((4, 128), f32),
+            pltpu.VMEM((KT, 128), f32),
             dma((1 + CHUNKS,)),
             dma((1 + CHUNKS,)),
             dma((2,)),
@@ -402,11 +542,17 @@
             dma((12,)),
         ],
         compiler_params=pltpu.CompilerParams(
-            collective_id=0, has_side_effects=True, vmem_limit_bytes=63 * 1024 * 1024
+            collective_id=0 if fast else 1, has_side_effects=True, vmem_limit_bytes=63 * 1024 * 1024
         ),
-        name="sinkhorn",
+        name="sinkhorn" if fast else "sinkhorn_log",
     )(x_feat.T, y_feat.T, a_logits.reshape(4, 128), b_logits.reshape(24, 128))
     return f.reshape(512), g.reshape(3072), loss.reshape(())
+
+
+def body(x_feat, y_feat, a_logits, b_logits):
+    args = x_feat, y_feat, a_logits, b_logits
+    f, g, loss = whole(True, *args)
+    return lax.cond(jnp.isfinite(loss), lambda *_: (f, g, loss), functools.partial(whole, False), *args)
 
 
 def solution(mesh):

time: 80.6 us -> 172 us (2.13)
  Pallas kernels: 76.2 us -> 166 us
    pallas_call x1 -> x2, Pallas kernels: 76.2 us -> 166 us  [whole(): pl.pallas_call(functools.partial(kernel, fast), out_shape=(jax.ShapeDtype...]
where the time goes in v4:
time: 172 us
  Pallas kernels  166 us (97%)
  between operations  3.17 us (2%)
  local copies, waits for them, and re-layouts  1.87 us (1%)
    pallas_call x2, Pallas kernels, whole(): pl.pallas_call(functools.partial(kernel, fast), out_shape=(jax.ShapeDtype...  166 us

profile of v4, /device:TPU:1, one launch (start us, length us, event | category | flops | bytes accessed | tf_op | source)
XLA Modules:
  0.0 171.5 jit_solution(3159731241367303890)
XLA Ops:
  0.6 0.0 copy-start.3
  0.6 0.7 copy-done.3
  1.3 0.0 copy-start
  1.3 0.0 copy-start.1
  1.3 0.0 copy-start.2
  1.3 96.9 %sinkhorn.1 = (f32[4,128]{1,0:T(4,128)S(1)}, f32[24,128]{1,0:T(8,128)S(1)}, f32[1,1]{1,0:T(1,128)}) custom-call(bf16[32,512]{1,0:T(8,128)(2,1)} %bitcast.14, bf16[8,3072]{1,0:T(8,128)(2,1)} %bitcast.12, f32[4,128]{1,0:T(4,128)S(1)} %bitcast.19, f32[24,128]{1,0:T(8,128)} %bitcast.16), custom_call_target="tpu_custom_call" | custom-call | tf_op jit(solution)/shard_map/sinkhorn/pallas_call | solution.py:491
  98.9 0.0 copy-done
  98.9 0.0 copy-done.1
  98.9 0.0 copy-done.2
  98.9 69.6 %conditional.1 = (f32[]{:T(128)}, f32[4,128]{1,0:T(4,128)S(1)}, f32[24,128]{1,0:T(8,128)S(1)}) conditional(s32[]{:T(128)} %convert_element_type.3, (bf16[512,32]{0,1:T(8,128)(2,1)S(1)}, bf16[3072,8]{0,1:T(8,128)(2,1)S(1)}, f32[512]{0:T(512)S(1)}, f32[3072]{0:T(1024)S(1)}) %tuple.28, (f32[4,128]{1,0:T(4,128)S(1)}, f32[24,128]{1,0:T(8,128)S(1)}, ...), branch_computations={%region_0.0_spmd, %region_1.0_spmd} | conditional | bytes 24 | solution.py:555
  98.9 69.4 %sinkhorn_log.1 = (f32[4,128]{1,0:T(4,128)S(1)}, f32[24,128]{1,0:T(8,128)S(1)}, f32[1,1]{1,0:T(1,128)}) custom-call(bf16[32,512]{1,0:T(8,128)(2,1)S(1)} %bitcast.15, bf16[8,3072]{1,0:T(8,128)(2,1)S(1)} %bitcast.13, f32[4,128]{1,0:T(4,128)S(1)} %bitcast.20, f32[24,128]{1,0:T(8,128)S(1)} %bitcast.17), custom_call_target="tpu_custom_call" | custom-call | tf_op jit(solution)/shard_map/cond/branch_0_fun/sinkhorn_log/pallas_call | solution.py:491
  168.5 0.6 copy.16
  169.1 0.6 copy.17
Async XLA Ops:
  0.6 0.7 copy-start.3
  1.3 97.6 %copy-start = (bf16[3072,8]{0,1:T(8,128)(2,1)S(1)}, bf16[3072,8]{0,1:T(8,128)(2,1)}, u32[]{:S(2)}) copy-start(bf16[3072,8]{0,1:T(8,128)(2,1)} %param.7) | copy-start | bytes 147460
  1.3 97.6 %copy-start.1 = (bf16[512,32]{0,1:T(8,128)(2,1)S(1)}, bf16[512,32]{0,1:T(8,128)(2,1)}, u32[]{:S(2)}) copy-start(bf16[512,32]{0,1:T(8,128)(2,1)} %param.6) | copy-start | bytes 98308
  1.3 97.6 %copy-start.2 = (f32[3072]{0:T(1024)S(1)}, f32[3072]{0:T(1024)}, u32[]{:S(2)}) copy-start(f32[3072]{0:T(1024)} %param.9) | copy-start | bytes 36868

commit v5 on v4

--- a/solution.py
+++ b/solution.py
@@ -77,7 +77,7 @@
 
 def kernel(
     fast, xt, yt, a, b, f_out, g_out, loss_out,
-    XT, XR, Y8, YM, S, VB, UB, ZB, AA, OWN_B, NA, NB, LA, LB, LBN, XSQ, YSQ, GM, GS, FX, GX, FL, GL, GH, FO, LO, FP, FM, LAM, BADR, BADC,
+    XT, XR, Y8, YM, S, PB, VB, UB, ZB, AA, OWN_B, NA, NB, LA, LB, LBN, XSQ, YSQ, GM, GS, FX, GX, FL, GL, GH, FO, LO, FP, FM, LAM, BADR, BADC,
     hsem, ysem, xsem, asem, nsem, local, fs, fr, gs, gr, ends,
 ):
     co = coords()
@@ -157,14 +157,14 @@
     def _():
         work(
             fast, co, row, col, xy, zed, xy_peers, z_peers, across, sibling, own, f_out, g_out, loss_out,
-            XT, XR, Y8, YM, S, VB, UB, ZB, AA, OWN_B, NA, NB, LA, LB, LBN, XSQ, YSQ, GM, GS, FX, GX, FL, GL, GH, FO, LO, FP, FM, LAM, BADR, BADC,
+            XT, XR, Y8, YM, S, PB, VB, UB, ZB, AA, OWN_B, NA, NB, LA, LB, LBN, XSQ, YSQ, GM, GS, FX, GX, FL, GL, GH, FO, LO, FP, FM, LAM, BADR, BADC,
             hsem, ysem, xsem, asem, nsem, fs, fr, gs, gr, ends,
         )
 
 
 def work(
     fast, co, row, col, xy, zed, xy_peers, z_peers, across, sibling, own, f_out, g_out, loss_out,
-    XT, XR, Y8, YM, S, VB, UB, ZB, AA, OWN_B, NA, NB, LA, LB, LBN, XSQ, YSQ, GM, GS, FX, GX, FL, GL, GH, FO, LO, FP, FM, LAM, BADR, BADC,
+    XT, XR, Y8, YM, S, PB, VB, UB, ZB, AA, OWN_B, NA, NB, LA, LB, LBN, XSQ, YSQ, GM, GS, FX, GX, FL, GL, GH, FO, LO, FP, FM, LAM, BADR, BADC,
     hsem, ysem, xsem, asem, nsem, fs, fr, gs, gr, ends,
 ):
     other = co["z"] * 4 + across["xl"] * 2
@@ -337,7 +337,7 @@
                     sums.append(
                         tree(
                             jnp.add,
-                            [S[at, k * 128 : (k + 1) * 128] * VB[:, k * 128 : (k + 1) * 128] for k in range(KT)],
+                            [PB[at, k * 128 : (k + 1) * 128] * VB[:, k * 128 : (k + 1) * 128] for k in range(KT)],
                         )
                     )
                 FX[t, h, xy, q : q + 1, :] = jnp.sum(jnp.concatenate(sums, axis=0).T, axis=0, keepdims=True)
@@ -371,15 +371,15 @@
                     z = [ZB[i : i + 8, :] for i in at]
                     for k in range(GROUP):
                         lanes = slice((k0 + k) * 128, (k0 + k + 1) * 128)
-                        terms = []
-                        for r in range(16):
-                            here = pl.ds(pl.multiple_of(h * 512 + at[r], 8), 8)
-                            p = S[here, lanes]
-                            if first:
-                                p = jnp.exp2(p + VB[:, lanes] - UB[at[r] : at[r] + 8, :])
-                                S[here, lanes] = p
-                            terms.append(p * z[r])
-                        sums[k] = sums[k] + tree(jnp.add, terms)
+                        here = [pl.ds(pl.multiple_of(h * 512 + i, 8), 8) for i in at]
+                        if first:
+                            p = [S[here[r], lanes] + VB[:, lanes] for r in range(16)]
+                            p = [jnp.exp2(p[r] - UB[at[r] : at[r] + 8, :]) for r in range(16)]
+                            for r in range(16):
+                                PB[here[r], lanes] = p[r]
+                        else:
+                            p = [PB[here[r], lanes] for r in range(16)]
+                        sums[k] = sums[k] + tree(jnp.add, [p[r] * z[r] for r in range(16)])
                 for k in range(GROUP):
                     GS[:, (k0 + k) * 128 : (k0 + k + 1) * 128] = sums[k]
             return 0
@@ -503,6 +503,7 @@
             pltpu.VMEM((CHUNKS, 32, 8, CHUNK), bf16),
             pltpu.VMEM((F, COLS), bf16),
             pltpu.VMEM((ROWS, COLS), f32),
+            pltpu.VMEM((ROWS, COLS) if fast else (8, 128), f32),
             pltpu.VMEM((8, COLS), f32),
             pltpu.VMEM((512, 128), f32),
             pltpu.VMEM((512, 128), f32),

time: 172 us -> 145 us (0.84)
  Pallas kernels: 166 us -> 140 us
    pallas_call x2, Pallas kernels: 166 us -> 140 us  [whole(): pl.pallas_call(functools.partial(kernel, fast), out_shape=(jax.ShapeDtype...]
where the time goes in v5:
time: 145 us
  Pallas kernels  140 us (97%)
  between operations  3.17 us (2%)
  local copies, waits for them, and re-layouts  1.87 us (1%)
    pallas_call x2, Pallas kernels, whole(): pl.pallas_call(functools.partial(kernel, fast), out_shape=(jax.ShapeDtype...  140 us

profile of v5, /device:TPU:1, one launch (start us, length us, event | category | flops | bytes accessed | tf_op | source)
XLA Modules:
  0.0 144.7 jit_solution(13538930638078893022)
XLA Ops:
  0.6 0.0 copy-start.3
  0.6 0.7 copy-done.3
  1.3 0.0 copy-start
  1.3 0.0 copy-start.1
  1.3 0.0 copy-start.2
  1.3 70.3 %sinkhorn.1 = (f32[4,128]{1,0:T(4,128)S(1)}, f32[24,128]{1,0:T(8,128)S(1)}, f32[1,1]{1,0:T(1,128)}) custom-call(bf16[32,512]{1,0:T(8,128)(2,1)} %bitcast.14, bf16[8,3072]{1,0:T(8,128)(2,1)} %bitcast.12, f32[4,128]{1,0:T(4,128)S(1)} %bitcast.19, f32[24,128]{1,0:T(8,128)} %bitcast.16), custom_call_target="tpu_custom_call" | custom-call | tf_op jit(solution)/shard_map/sinkhorn/pallas_call | solution.py:491
  72.4 0.0 copy-done
  72.4 0.0 copy-done.1
  72.4 0.0 copy-done.2
  72.4 69.3 %conditional.1 = (f32[]{:T(128)}, f32[4,128]{1,0:T(4,128)S(1)}, f32[24,128]{1,0:T(8,128)S(1)}) conditional(s32[]{:T(128)} %convert_element_type.3, (bf16[512,32]{0,1:T(8,128)(2,1)S(1)}, bf16[3072,8]{0,1:T(8,128)(2,1)S(1)}, f32[512]{0:T(512)S(1)}, f32[3072]{0:T(1024)S(1)}) %tuple.28, (f32[4,128]{1,0:T(4,128)S(1)}, f32[24,128]{1,0:T(8,128)S(1)}, ...), branch_computations={%region_0.0_spmd, %region_1.0_spmd} | conditional | bytes 24 | solution.py:556
  72.4 69.3 %sinkhorn_log.1 = (f32[4,128]{1,0:T(4,128)S(1)}, f32[24,128]{1,0:T(8,128)S(1)}, f32[1,1]{1,0:T(1,128)}) custom-call(bf16[32,512]{1,0:T(8,128)(2,1)S(1)} %bitcast.15, bf16[8,3072]{1,0:T(8,128)(2,1)S(1)} %bitcast.13, f32[4,128]{1,0:T(4,128)S(1)} %bitcast.20, f32[24,128]{1,0:T(8,128)S(1)} %bitcast.17), custom_call_target="tpu_custom_call" | custom-call | tf_op jit(solution)/shard_map/cond/branch_0_fun/sinkhorn_log/pallas_call | solution.py:491
  141.7 0.6 copy.16
  142.3 0.6 copy.17
Async XLA Ops:
  0.6 0.7 copy-start.3
  1.3 71.0 %copy-start = (bf16[3072,8]{0,1:T(8,128)(2,1)S(1)}, bf16[3072,8]{0,1:T(8,128)(2,1)}, u32[]{:S(2)}) copy-start(bf16[3072,8]{0,1:T(8,128)(2,1)} %param.7) | copy-start | bytes 147460
  1.3 71.0 %copy-start.1 = (bf16[512,32]{0,1:T(8,128)(2,1)S(1)}, bf16[512,32]{0,1:T(8,128)(2,1)}, u32[]{:S(2)}) copy-start(bf16[512,32]{0,1:T(8,128)(2,1)} %param.6) | copy-start | bytes 98308
  1.3 71.1 %copy-start.2 = (f32[3072]{0:T(1024)S(1)}, f32[3072]{0:T(1024)}, u32[]{:S(2)}) copy-start(f32[3072]{0:T(1024)} %param.9) | copy-start | bytes 36868

commit v6 on v5

--- a/solution.py
+++ b/solution.py
@@ -18,7 +18,7 @@
 ROWS, COLS = 2048, 1536
 PARTS = 4
 KT = COLS // 128
-CHUNKS = 3
+CHUNKS = 2
 CHUNK = COLS // CHUNKS
 GROUP = 4
 
@@ -126,6 +126,12 @@
 
     pl.semaphore_wait(barrier, len(xy_offsets) + len(z_offsets) + 1)
 
+    send(a, AA.at[row % 4], asem.at[0], asem.at[1], across)
+
+    @pl.when(helper)
+    def _():
+        send(a, AA.at[row % 4], asem.at[0], asem.at[1], sibling)
+
     for n in range(CHUNKS):
         send(cut(across["xl"], n), Y8.at[n, row], hsem.at[0], hsem.at[1 + n], across)
     for n in range(CHUNKS):
@@ -133,14 +139,12 @@
             send(cut(co["xl"], n), Y8.at[n, row], ysem.at[0], ysem.at[1 + n], t)
     for t in xy_peers:
         send(xt, XT.at[row % 4 * 8 + col], xsem.at[0], xsem.at[1], t)
-    send(a, AA.at[row % 4], asem.at[0], asem.at[1], across)
 
     @pl.when(helper)
     def _():
         for n in range(CHUNKS):
             send(cut(co["xl"], n), Y8.at[n, row], ysem.at[0], ysem.at[1 + n], sibling)
         send(xt, XT.at[row % 4 * 8 + col], xsem.at[0], xsem.at[1], sibling)
-        send(a, AA.at[row % 4], asem.at[0], asem.at[1], sibling)
         drain(Y8.at[0, pl.ds(0, CHUNKS)], hsem.at[0])
         drain(Y8.at[0, pl.ds(0, CHUNKS * 8)], ysem.at[0])
         drain(XT.at[pl.ds(0, 16)], xsem.at[0])
@@ -192,8 +196,6 @@
     for p in range(16):
         x = XT[p // 4 * 8 : p // 4 * 8 + 8, :, pl.ds((p % 4) * 128, 128)].reshape(F, 128)
         XR[p * 128 : (p + 1) * 128, :] = x.T
-        x = x.astype(jnp.float32)
-        XSQ[p : p + 1, :] = jnp.sum(x * x, axis=0, keepdims=True)
 
     def set_v(v, first, count):
         for k in range(count):
@@ -229,22 +231,18 @@
         mine = slice(n * tiles_in, (n + 1) * tiles_in)
         set_v(LB[mine] - YSQ[mine] * (LOG2E / F / EPS), n * tiles_in, tiles_in)
 
-        def multiply(p, _):
-            at = pl.ds(pl.multiple_of(p * 128, 128), 128)
-            inner = jnp.dot(XR[at, :], YM[:, span], preferred_element_type=jnp.float32)
-            S[at, span] = inner * scale
-            return 0
-
-        lax.fori_loop(0, 16, multiply, 0, unroll=4)
-
         def first_rows(h, _):
             for q in range(4):
+                block = pl.ds(pl.multiple_of(h * 512 + q * 128, 128), 128)
+                inner = jnp.dot(XR[block, :], YM[:, span], preferred_element_type=jnp.float32) * scale
+                S[block, span] = inner
                 peaks, masses = [], []
                 for r in range(16):
                     at = pl.ds(pl.multiple_of(h * 512 + q * 128 + r * 8, 8), 8)
                     tiles = [
-                        S[at, k * 128 : (k + 1) * 128] + VB[:, k * 128 : (k + 1) * 128]
-                        for k in range(n * tiles_in, (n + 1) * tiles_in)
+                        inner[r * 8 : (r + 1) * 8, k * 128 : (k + 1) * 128]
+                        + VB[:, (n * tiles_in + k) * 128 : (n * tiles_in + k + 1) * 128]
+                        for k in range(tiles_in)
                     ]
                     if n:
                         before = FP[at, :]
@@ -394,6 +392,10 @@
         good = jnp.logical_and(total >= 2.0**-65, w <= 2.0**45)
         BADC[...] = jnp.maximum(BADC[...], jnp.where(good, 0.0, 1.0))
         return w
+
+    for p in range(16):
+        x = XT[p // 4 * 8 : p // 4 * 8 + 8, :, pl.ds((p % 4) * 128, 128)].reshape(F, 128).astype(jnp.float32)
+        XSQ[p : p + 1, :] = jnp.sum(x * x, axis=0, keepdims=True)
 
     drain(NB.at[pl.ds(0, 15)], nsem.at[1])
     drain(NA.at[pl.ds(0, 7)], nsem.at[3])

time: 145 us -> 140 us (0.966)
  Pallas kernels: 140 us -> 134 us
    pallas_call x2, Pallas kernels: 140 us -> 134 us  [whole(): pl.pallas_call(functools.partial(kernel, fast), out_shape=(jax.ShapeDtype...]
where the time goes in v6:
time: 140 us
  Pallas kernels  134 us (96%)
  between operations  3.17 us (2%)
  local copies, waits for them, and re-layouts  1.87 us (1%)
    pallas_call x2, Pallas kernels, whole(): pl.pallas_call(functools.partial(kernel, fast), out_shape=(jax.ShapeDtype...  134 us

profile of v6, /device:TPU:1, one launch (start us, length us, event | category | flops | bytes accessed | tf_op | source)
XLA Modules:
  0.0 139.5 jit_solution(16696382144725623713)
XLA Ops:
  0.6 0.0 copy-start.3
  0.6 0.7 copy-done.3
  1.3 0.0 copy-start
  1.3 0.0 copy-start.1
  1.3 0.0 copy-start.2
  1.3 67.6 %sinkhorn.1 = (f32[4,128]{1,0:T(4,128)S(1)}, f32[24,128]{1,0:T(8,128)S(1)}, f32[1,1]{1,0:T(1,128)}) custom-call(bf16[32,512]{1,0:T(8,128)(2,1)} %bitcast.14, bf16[8,3072]{1,0:T(8,128)(2,1)} %bitcast.12, f32[4,128]{1,0:T(4,128)S(1)} %bitcast.19, f32[24,128]{1,0:T(8,128)} %bitcast.16), custom_call_target="tpu_custom_call" | custom-call | tf_op jit(solution)/shard_map/sinkhorn/pallas_call | solution.py:493
  69.6 0.0 copy-done
  69.6 0.0 copy-done.1
  69.6 0.0 copy-done.2
  69.6 66.9 %conditional.1 = (f32[]{:T(128)}, f32[4,128]{1,0:T(4,128)S(1)}, f32[24,128]{1,0:T(8,128)S(1)}) conditional(s32[]{:T(128)} %convert_element_type.3, (bf16[512,32]{0,1:T(8,128)(2,1)S(1)}, bf16[3072,8]{0,1:T(8,128)(2,1)S(1)}, f32[512]{0:T(512)S(1)}, f32[3072]{0:T(1024)S(1)}) %tuple.28, (f32[4,128]{1,0:T(4,128)S(1)}, f32[24,128]{1,0:T(8,128)S(1)}, ...), branch_computations={%region_0.0_spmd, %region_1.0_spmd} | conditional | bytes 24 | solution.py:558
  69.7 66.9 %sinkhorn_log.1 = (f32[4,128]{1,0:T(4,128)S(1)}, f32[24,128]{1,0:T(8,128)S(1)}, f32[1,1]{1,0:T(1,128)}) custom-call(bf16[32,512]{1,0:T(8,128)(2,1)S(1)} %bitcast.15, bf16[8,3072]{1,0:T(8,128)(2,1)S(1)} %bitcast.13, f32[4,128]{1,0:T(4,128)S(1)} %bitcast.20, f32[24,128]{1,0:T(8,128)S(1)} %bitcast.17), custom_call_target="tpu_custom_call" | custom-call | tf_op jit(solution)/shard_map/cond/branch_0_fun/sinkhorn_log/pallas_call | solution.py:493
  136.5 0.6 copy.16
  137.1 0.6 copy.17
Async XLA Ops:
  0.6 0.7 copy-start.3
  1.3 68.3 %copy-start = (bf16[3072,8]{0,1:T(8,128)(2,1)S(1)}, bf16[3072,8]{0,1:T(8,128)(2,1)}, u32[]{:S(2)}) copy-start(bf16[3072,8]{0,1:T(8,128)(2,1)} %param.7) | copy-start | bytes 147460
  1.3 68.3 %copy-start.1 = (bf16[512,32]{0,1:T(8,128)(2,1)S(1)}, bf16[512,32]{0,1:T(8,128)(2,1)}, u32[]{:S(2)}) copy-start(bf16[512,32]{0,1:T(8,128)(2,1)} %param.6) | copy-start | bytes 98308
  1.3 68.3 %copy-start.2 = (f32[3072]{0:T(1024)S(1)}, f32[3072]{0:T(1024)}, u32[]{:S(2)}) copy-start(f32[3072]{0:T(1024)} %param.9) | copy-start | bytes 36868

commit v7 on v6

--- a/solution.py
+++ b/solution.py
@@ -77,7 +77,7 @@
 
 def kernel(
     fast, xt, yt, a, b, f_out, g_out, loss_out,
-    XT, XR, Y8, YM, S, PB, VB, UB, ZB, AA, OWN_B, NA, NB, LA, LB, LBN, XSQ, YSQ, GM, GS, FX, GX, FL, GL, GH, FO, LO, FP, FM, LAM, BADR, BADC,
+    XT, XR, Y8, YM, S, PB, VB, UB, ZB, AA, OWN_B, NA, NB, LA, LB, LBN, XSQ, YSQ, GM, GS, FX, GX, FL, GL, GH, FO, LO, FP, FM, LAM, TOP, RHO, BADR, BADC,
     hsem, ysem, xsem, asem, nsem, local, fs, fr, gs, gr, ends,
 ):
     co = coords()
@@ -101,7 +101,7 @@
 
     @pl.when(worker)
     def _():
-        for o in xy_offsets + z_offsets:
+        for o in sorted(xy_offsets + z_offsets, key=lambda o: -hops(o)):
             greet(at_offset(co, o, 0))
             greet(at_offset(co, o, 1))
         greet(sibling)
@@ -161,14 +161,14 @@
     def _():
         work(
             fast, co, row, col, xy, zed, xy_peers, z_peers, across, sibling, own, f_out, g_out, loss_out,
-            XT, XR, Y8, YM, S, PB, VB, UB, ZB, AA, OWN_B, NA, NB, LA, LB, LBN, XSQ, YSQ, GM, GS, FX, GX, FL, GL, GH, FO, LO, FP, FM, LAM, BADR, BADC,
+            XT, XR, Y8, YM, S, PB, VB, UB, ZB, AA, OWN_B, NA, NB, LA, LB, LBN, XSQ, YSQ, GM, GS, FX, GX, FL, GL, GH, FO, LO, FP, FM, LAM, TOP, RHO, BADR, BADC,
             hsem, ysem, xsem, asem, nsem, fs, fr, gs, gr, ends,
         )
 
 
 def work(
     fast, co, row, col, xy, zed, xy_peers, z_peers, across, sibling, own, f_out, g_out, loss_out,
-    XT, XR, Y8, YM, S, PB, VB, UB, ZB, AA, OWN_B, NA, NB, LA, LB, LBN, XSQ, YSQ, GM, GS, FX, GX, FL, GL, GH, FO, LO, FP, FM, LAM, BADR, BADC,
+    XT, XR, Y8, YM, S, PB, VB, UB, ZB, AA, OWN_B, NA, NB, LA, LB, LBN, XSQ, YSQ, GM, GS, FX, GX, FL, GL, GH, FO, LO, FP, FM, LAM, TOP, RHO, BADR, BADC,
     hsem, ysem, xsem, asem, nsem, fs, fr, gs, gr, ends,
 ):
     other = co["z"] * 4 + across["xl"] * 2
@@ -192,11 +192,6 @@
     for t in z_peers:
         send(NA.at[zed], NA.at[zed], nsem.at[2], nsem.at[3], t)
 
-    drain(XT.at[pl.ds(0, 31)], xsem.at[1])
-    for p in range(16):
-        x = XT[p // 4 * 8 : p // 4 * 8 + 8, :, pl.ds((p % 4) * 128, 128)].reshape(F, 128)
-        XR[p * 128 : (p + 1) * 128, :] = x.T
-
     def set_v(v, first, count):
         for k in range(count):
             at = first + k
@@ -206,7 +201,7 @@
         peak = jnp.concatenate(peaks, axis=0).T
         mass = jnp.concatenate(masses, axis=0).T
         top = jnp.max(peak, axis=0, keepdims=True)
-        return top + jnp.log2(jnp.sum(mass * jnp.exp2(peak - top), axis=0, keepdims=True))
+        return top, top + jnp.log2(jnp.sum(mass * jnp.exp2(peak - top), axis=0, keepdims=True))
 
     def send_rows(t, h):
         for peer in xy_peers:
@@ -231,10 +226,18 @@
         mine = slice(n * tiles_in, (n + 1) * tiles_in)
         set_v(LB[mine] - YSQ[mine] * (LOG2E / F / EPS), n * tiles_in, tiles_in)
 
+        if n == 0:
+            drain(XT.at[pl.ds(0, 31)], xsem.at[1])
+
         def first_rows(h, _):
             for q in range(4):
                 block = pl.ds(pl.multiple_of(h * 512 + q * 128, 128), 128)
-                inner = jnp.dot(XR[block, :], YM[:, span], preferred_element_type=jnp.float32) * scale
+                if n:
+                    x = XR[block, :]
+                else:
+                    x = XT[pl.ds(pl.multiple_of(h * 8, 8), 8), :, q * 128 : (q + 1) * 128].reshape(F, 128).T
+                    XR[block, :] = x
+                inner = jnp.dot(x, YM[:, span], preferred_element_type=jnp.float32) * scale
                 S[block, span] = inner
                 peaks, masses = [], []
                 for r in range(16):
@@ -258,7 +261,8 @@
                     peaks.append(peak)
                     masses.append(mass)
                 if n == CHUNKS - 1:
-                    FX[0, h, xy, q : q + 1, :] = over_lanes(peaks, masses)
+                    top, FX[0, h, xy, q : q + 1, :] = over_lanes(peaks, masses)
+                    TOP[pl.ds(h * 4 + q, 1), :] = top
             if n == CHUNKS - 1:
                 send_rows(0, h)
             return 0
@@ -275,7 +279,7 @@
                     peak = functools.reduce(jnp.maximum, tiles)
                     peaks.append(peak)
                     masses.append(functools.reduce(jnp.add, [jnp.exp2(s - peak) for s in tiles]))
-                FX[t, h, xy, q : q + 1, :] = over_lanes(peaks, masses)
+                FX[t, h, xy, q : q + 1, :] = over_lanes(peaks, masses)[1]
             send_rows(t, h)
             return 0
 
@@ -338,7 +342,8 @@
                             [PB[at, k * 128 : (k + 1) * 128] * VB[:, k * 128 : (k + 1) * 128] for k in range(KT)],
                         )
                     )
-                FX[t, h, xy, q : q + 1, :] = jnp.sum(jnp.concatenate(sums, axis=0).T, axis=0, keepdims=True)
+                total = jnp.sum(jnp.concatenate(sums, axis=0).T, axis=0, keepdims=True)
+                FX[t, h, xy, q : q + 1, :] = total * RHO[pl.ds(h * 4 + q, 1), :]
             send_rows(t, h)
             return 0
 
@@ -352,14 +357,14 @@
             if first:
                 lam = lse(FX[t, h])
                 LAM[rows, :] = lam - LBN[...]
+                RHO[rows, :] = jnp.exp2(TOP[rows, :] - lam)
                 zs = mass_a
-                for q in range(4):
-                    UB[q * 128 : (q + 1) * 128, :] = jnp.broadcast_to(lam[q : q + 1, :], (128, 128)).T
             else:
                 total = jnp.sum(FX[t, h], axis=0)
                 zs = mass_a / total
                 good = jnp.logical_and(total >= 2.0**-35, zs <= 2.0**20)
                 BADR[...] = jnp.maximum(BADR[...], jnp.where(good, 0.0, 1.0))
+            zs = zs * RHO[rows, :]
             for q in range(4):
                 ZB[q * 128 : (q + 1) * 128, :] = jnp.broadcast_to(zs[q : q + 1, :], (128, 128)).T
             for k0 in range(0, KT, GROUP):
@@ -370,14 +375,7 @@
                     for k in range(GROUP):
                         lanes = slice((k0 + k) * 128, (k0 + k + 1) * 128)
                         here = [pl.ds(pl.multiple_of(h * 512 + i, 8), 8) for i in at]
-                        if first:
-                            p = [S[here[r], lanes] + VB[:, lanes] for r in range(16)]
-                            p = [jnp.exp2(p[r] - UB[at[r] : at[r] + 8, :]) for r in range(16)]
-                            for r in range(16):
-                                PB[here[r], lanes] = p[r]
-                        else:
-                            p = [PB[here[r], lanes] for r in range(16)]
-                        sums[k] = sums[k] + tree(jnp.add, [p[r] * z[r] for r in range(16)])
+                        sums[k] = sums[k] + tree(jnp.add, [PB[here[r], lanes] * z[r] for r in range(16)])
                 for k in range(GROUP):
                     GS[:, (k0 + k) * 128 : (k0 + k + 1) * 128] = sums[k]
             return 0
@@ -393,6 +391,23 @@
         BADC[...] = jnp.maximum(BADC[...], jnp.where(good, 0.0, 1.0))
         return w
 
+    def exponentials(h, _):
+        tops = TOP[pl.ds(pl.multiple_of(h * 4, 4), 4), :]
+        for q in range(4):
+            UB[q * 128 : (q + 1) * 128, :] = jnp.broadcast_to(tops[q : q + 1, :], (128, 128)).T
+        for q in range(4):
+            for k in range(KT):
+                lanes = slice(k * 128, (k + 1) * 128)
+                at = [q * 128 + r * 8 for r in range(16)]
+                here = [pl.ds(pl.multiple_of(h * 512 + i, 8), 8) for i in at]
+                p = [S[here[r], lanes] + VB[:, lanes] for r in range(16)]
+                p = [jnp.exp2(p[r] - UB[at[r] : at[r] + 8, :]) for r in range(16)]
+                for r in range(16):
+                    PB[here[r], lanes] = p[r]
+        return 0
+
+    if fast:
+        lax.fori_loop(0, PARTS, exponentials, 0)
     for p in range(16):
         x = XT[p // 4 * 8 : p // 4 * 8 + 8, :, pl.ds((p % 4) * 128, 128)].reshape(F, 128).astype(jnp.float32)
         XSQ[p : p + 1, :] = jnp.sum(x * x, axis=0, keepdims=True)
@@ -530,6 +545,8 @@
             pltpu.VMEM((ROWS, 128), f32),
             pltpu.VMEM((ROWS, 128), f32),
             pltpu.VMEM((16, 128), f32),
+            pltpu.VMEM((16, 128), f32),
+            pltpu.VMEM((16, 128), f32),
             pltpu.VMEM((4, 128), f32),
             pltpu.VMEM((KT, 128), f32),
             dma((1 + CHUNKS,)),

time: 140 us -> 138 us (0.986)
  Pallas kernels: 134 us -> 132 us
    pallas_call x2, Pallas kernels: 134 us -> 132 us  [whole(): pl.pallas_call(functools.partial(kernel, fast), out_shape=(jax.ShapeDtype...]
where the time goes in v7:
time: 138 us; the launch traced here: 137 us
  Pallas kernels  132 us (96%)
  between operations  3.17 us (2%)
  local copies, waits for them, and re-layouts  1.87 us (1%)
    pallas_call x2, Pallas kernels, whole(): pl.pallas_call(functools.partial(kernel, fast), out_shape=(jax.ShapeDtype...  132 us

profile of v7, /device:TPU:1, one launch (start us, length us, event | category | flops | bytes accessed | tf_op | source)
XLA Modules:
  0.0 137.4 jit_solution(11774745321450694709)
XLA Ops:
  0.6 0.0 copy-start.3
  0.6 0.7 copy-done.3
  1.3 0.0 copy-start
  1.3 0.0 copy-start.1
  1.3 0.0 copy-start.2
  1.3 66.2 %sinkhorn.1 = (f32[4,128]{1,0:T(4,128)S(1)}, f32[24,128]{1,0:T(8,128)S(1)}, f32[1,1]{1,0:T(1,128)}) custom-call(bf16[32,512]{1,0:T(8,128)(2,1)} %bitcast.14, bf16[8,3072]{1,0:T(8,128)(2,1)} %bitcast.12, f32[4,128]{1,0:T(4,128)S(1)} %bitcast.19, f32[24,128]{1,0:T(8,128)} %bitcast.16), custom_call_target="tpu_custom_call" | custom-call | tf_op jit(solution)/shard_map/sinkhorn/pallas_call | solution.py:508
  68.2 0.0 copy-done
  68.3 0.0 copy-done.1
  68.3 0.0 copy-done.2
  68.3 66.1 %conditional.1 = (f32[]{:T(128)}, f32[4,128]{1,0:T(4,128)S(1)}, f32[24,128]{1,0:T(8,128)S(1)}) conditional(s32[]{:T(128)} %convert_element_type.3, (bf16[512,32]{0,1:T(8,128)(2,1)S(1)}, bf16[3072,8]{0,1:T(8,128)(2,1)S(1)}, f32[512]{0:T(512)S(1)}, f32[3072]{0:T(1024)S(1)}) %tuple.28, (f32[4,128]{1,0:T(4,128)S(1)}, f32[24,128]{1,0:T(8,128)S(1)}, ...), branch_computations={%region_0.0_spmd, %region_1.0_spmd} | conditional | bytes 24 | solution.py:575
  68.3 66.1 %sinkhorn_log.1 = (f32[4,128]{1,0:T(4,128)S(1)}, f32[24,128]{1,0:T(8,128)S(1)}, f32[1,1]{1,0:T(1,128)}) custom-call(bf16[32,512]{1,0:T(8,128)(2,1)S(1)} %bitcast.15, bf16[8,3072]{1,0:T(8,128)(2,1)S(1)} %bitcast.13, f32[4,128]{1,0:T(4,128)S(1)} %bitcast.20, f32[24,128]{1,0:T(8,128)S(1)} %bitcast.17), custom_call_target="tpu_custom_call" | custom-call | tf_op jit(solution)/shard_map/cond/branch_0_fun/sinkhorn_log/pallas_call | solution.py:508
  134.4 0.6 copy.16
  135.0 0.6 copy.17
Async XLA Ops:
  0.6 0.7 copy-start.3
  1.3 66.9 %copy-start = (bf16[3072,8]{0,1:T(8,128)(2,1)S(1)}, bf16[3072,8]{0,1:T(8,128)(2,1)}, u32[]{:S(2)}) copy-start(bf16[3072,8]{0,1:T(8,128)(2,1)} %param.7) | copy-start | bytes 147460
  1.3 66.9 %copy-start.1 = (bf16[512,32]{0,1:T(8,128)(2,1)S(1)}, bf16[512,32]{0,1:T(8,128)(2,1)}, u32[]{:S(2)}) copy-start(bf16[512,32]{0,1:T(8,128)(2,1)} %param.6) | copy-start | bytes 98308
  1.3 67.0 %copy-start.2 = (f32[3072]{0:T(1024)S(1)}, f32[3072]{0:T(1024)}, u32[]{:S(2)}) copy-start(f32[3072]{0:T(1024)} %param.9) | copy-start | bytes 36868

commit v8 on v7

--- a/solution.py
+++ b/solution.py
@@ -77,7 +77,7 @@
 
 def kernel(
     fast, xt, yt, a, b, f_out, g_out, loss_out,
-    XT, XR, Y8, YM, S, PB, VB, UB, ZB, AA, OWN_B, NA, NB, LA, LB, LBN, XSQ, YSQ, GM, GS, FX, GX, FL, GL, GH, FO, LO, FP, FM, LAM, TOP, RHO, BADR, BADC,
+    XT, XR, Y8, YM, S, PB, VB, UB, ZB, AA, OWN_B, NA, NB, LA, LB, LBN, XSQ, YSQ, GM, GS, FX, GX, FL, GL, GH, FO, LO, FP, FM, LAM, TOP, RHO, EA, EAR, EB, BADR, BADC,
     hsem, ysem, xsem, asem, nsem, local, fs, fr, gs, gr, ends,
 ):
     co = coords()
@@ -161,14 +161,14 @@
     def _():
         work(
             fast, co, row, col, xy, zed, xy_peers, z_peers, across, sibling, own, f_out, g_out, loss_out,
-            XT, XR, Y8, YM, S, PB, VB, UB, ZB, AA, OWN_B, NA, NB, LA, LB, LBN, XSQ, YSQ, GM, GS, FX, GX, FL, GL, GH, FO, LO, FP, FM, LAM, TOP, RHO, BADR, BADC,
+            XT, XR, Y8, YM, S, PB, VB, UB, ZB, AA, OWN_B, NA, NB, LA, LB, LBN, XSQ, YSQ, GM, GS, FX, GX, FL, GL, GH, FO, LO, FP, FM, LAM, TOP, RHO, EA, EAR, EB, BADR, BADC,
             hsem, ysem, xsem, asem, nsem, fs, fr, gs, gr, ends,
         )
 
 
 def work(
     fast, co, row, col, xy, zed, xy_peers, z_peers, across, sibling, own, f_out, g_out, loss_out,
-    XT, XR, Y8, YM, S, PB, VB, UB, ZB, AA, OWN_B, NA, NB, LA, LB, LBN, XSQ, YSQ, GM, GS, FX, GX, FL, GL, GH, FO, LO, FP, FM, LAM, TOP, RHO, BADR, BADC,
+    XT, XR, Y8, YM, S, PB, VB, UB, ZB, AA, OWN_B, NA, NB, LA, LB, LBN, XSQ, YSQ, GM, GS, FX, GX, FL, GL, GH, FO, LO, FP, FM, LAM, TOP, RHO, EA, EAR, EB, BADR, BADC,
     hsem, ysem, xsem, asem, nsem, fs, fr, gs, gr, ends,
 ):
     other = co["z"] * 4 + across["xl"] * 2
@@ -353,18 +353,18 @@
         def part(h, _):
             drain(FX.at[t, h, pl.ds(0, 15)], fr.at[t, h])
             rows = pl.ds(pl.multiple_of(h * 4, 4), 4)
-            mass_a = jnp.exp2(LA[rows, :])
             if first:
                 lam = lse(FX[t, h])
                 LAM[rows, :] = lam - LBN[...]
-                RHO[rows, :] = jnp.exp2(TOP[rows, :] - lam)
-                zs = mass_a
+                rho = jnp.exp2(TOP[rows, :] - lam)
+                RHO[rows, :] = rho
+                zs = EA[rows, :] * rho
+                EAR[rows, :] = zs
             else:
                 total = jnp.sum(FX[t, h], axis=0)
-                zs = mass_a / total
-                good = jnp.logical_and(total >= 2.0**-35, zs <= 2.0**20)
+                zs = EAR[rows, :] / total
+                good = jnp.logical_and(total >= 2.0**-35, EA[rows, :] <= 2.0**20 * total)
                 BADR[...] = jnp.maximum(BADR[...], jnp.where(good, 0.0, 1.0))
-            zs = zs * RHO[rows, :]
             for q in range(4):
                 ZB[q * 128 : (q + 1) * 128, :] = jnp.broadcast_to(zs[q : q + 1, :], (128, 128)).T
             for k0 in range(0, KT, GROUP):
@@ -386,7 +386,7 @@
             GX[t, zed, k : k + 1, :] = jnp.sum(GS[:, k * 128 : (k + 1) * 128], axis=0, keepdims=True)
         swap_columns(t)
         total = jnp.sum(GX[t], axis=0)
-        w = jnp.exp2(LB[...]) / total
+        w = EB[...] / total
         good = jnp.logical_and(total >= 2.0**-65, w <= 2.0**45)
         BADC[...] = jnp.maximum(BADC[...], jnp.where(good, 0.0, 1.0))
         return w
@@ -419,6 +419,8 @@
     LB[...] = LB[...] - log_b_norm
     LA[...] = LA[...] - log_a_norm
     LBN[...] = log_b_norm
+    EA[...] = jnp.exp2(LA[...])
+    EB[...] = jnp.exp2(LB[...])
     BADR[...] = jnp.zeros(BADR.shape, jnp.float32)
     BADC[...] = jnp.zeros(BADC.shape, jnp.float32)
     last = ITERS - 1
@@ -547,6 +549,9 @@
             pltpu.VMEM((16, 128), f32),
             pltpu.VMEM((16, 128), f32),
             pltpu.VMEM((16, 128), f32),
+            pltpu.VMEM((16, 128), f32),
+            pltpu.VMEM((16, 128), f32),
+            pltpu.VMEM((KT, 128), f32),
             pltpu.VMEM((4, 128), f32),
             pltpu.VMEM((KT, 128), f32),
             dma((1 + CHUNKS,)),
@@ -562,7 +567,7 @@
             dma((12,)),
         ],
         compiler_params=pltpu.CompilerParams(
-            collective_id=0 if fast else 1, has_side_effects=True, vmem_limit_bytes=63 * 1024 * 1024
+            collective_id=0 if fast else 1, has_side_effects=True, vmem_limit_bytes=64 * 1024 * 1024 - 24 * 1024
         ),
         name="sinkhorn" if fast else "sinkhorn_log",
     )(x_feat.T, y_feat.T, a_logits.reshape(4, 128), b_logits.reshape(24, 128))

time: 138 us -> 138 us (level)
  no operation moved by 1% of the time
where the time goes in v8:
time: 138 us
  Pallas kernels  133 us (96%)
  between operations  2.9 us (2%)
  local copies, waits for them, and re-layouts  1.87 us (1%)
    pallas_call x2, Pallas kernels, whole(): pl.pallas_call(functools.partial(kernel, fast), out_shape=(jax.ShapeDtype...  133 us

profile of v8, /device:TPU:1, one launch (start us, length us, event | category | flops | bytes accessed | tf_op | source)
XLA Modules:
  0.0 137.7 jit_solution(18131916966772542194)
XLA Ops:
  0.6 66.4 %sinkhorn.1 = (f32[4,128]{1,0:T(4,128)}, f32[24,128]{1,0:T(8,128)}, f32[1,1]{1,0:T(1,128)}) custom-call(bf16[32,512]{1,0:T(8,128)(2,1)} %bitcast.14, bf16[8,3072]{1,0:T(8,128)(2,1)} %bitcast.12, f32[4,128]{1,0:T(4,128)} %bitcast.19, f32[24,128]{1,0:T(8,128)} %bitcast.16), custom_call_target="tpu_custom_call" | custom-call | tf_op jit(solution)/shard_map/sinkhorn/pallas_call | solution.py:510
  67.6 66.4 %conditional.1 = (f32[]{:T(128)}, f32[4,128]{1,0:T(4,128)}, f32[24,128]{1,0:T(8,128)}) conditional(s32[]{:T(128)} %convert_element_type.3, (bf16[512,32]{0,1:T(8,128)(2,1)}, bf16[3072,8]{0,1:T(8,128)(2,1)}, f32[512]{0:T(512)}, f32[3072]{0:T(1024)}) %tuple.16, (f32[4,128]{1,0:T(4,128)}, f32[24,128]{1,0:T(8,128)}, f32[]{:T(128)}) %tuple.17), branch_computations={%region_0.0_spmd, %region_1.0_spmd} | conditional | bytes 24 | solution.py:580
  67.6 66.4 %sinkhorn_log.1 = (f32[4,128]{1,0:T(4,128)}, f32[24,128]{1,0:T(8,128)}, f32[1,1]{1,0:T(1,128)}) custom-call(bf16[32,512]{1,0:T(8,128)(2,1)} %bitcast.15, bf16[8,3072]{1,0:T(8,128)(2,1)} %bitcast.13, f32[4,128]{1,0:T(4,128)} %bitcast.20, f32[24,128]{1,0:T(8,128)} %bitcast.17), custom_call_target="tpu_custom_call" | custom-call | tf_op jit(solution)/shard_map/cond/branch_0_fun/sinkhorn_log/pallas_call | solution.py:510
  134.1 0.0 copy-start
  134.1 1.3 copy.16
  135.4 0.0 copy-done
  135.4 0.6 copy.17
Async XLA Ops:
  134.1 1.3 copy-start

commit v9 on v8

--- a/solution.py
+++ b/solution.py
@@ -77,7 +77,7 @@
 
 def kernel(
     fast, xt, yt, a, b, f_out, g_out, loss_out,
-    XT, XR, Y8, YM, S, PB, VB, UB, ZB, AA, OWN_B, NA, NB, LA, LB, LBN, XSQ, YSQ, GM, GS, FX, GX, FL, GL, GH, FO, LO, FP, FM, LAM, TOP, RHO, EA, EAR, EB, BADR, BADC,
+    XT, XR, Y8, YM, S, PB, VB, UB, ZB, AA, OWN_B, NA, NB, LA, LB, LBN, XSQ, YSQ, GM, GS, FX, GX, FL, GL, GH, FO, FP, FM, LAM, TOP, RHO, EA, EAR, EB, BADR, BADC,
     hsem, ysem, xsem, asem, nsem, local, fs, fr, gs, gr, ends,
 ):
     co = coords()
@@ -151,24 +151,31 @@
         drain(AA.at[pl.ds(0, 2)], asem.at[0])
         drain(FO, ends.at[5])
         drain(GH, ends.at[7])
-        drain(LO, ends.at[9])
+        drain(GL, ends.at[1])
+        drain(FL, ends.at[11])
         f_out[...] = FO[...]
         g_out[:KT] = GH[0]
         g_out[KT:] = GH[1]
-        loss_out[...] = LO[0:1, 0:1]
+        loss_out[...] = objective(FL, GL)
 
     @pl.when(worker)
     def _():
         work(
             fast, co, row, col, xy, zed, xy_peers, z_peers, across, sibling, own, f_out, g_out, loss_out,
-            XT, XR, Y8, YM, S, PB, VB, UB, ZB, AA, OWN_B, NA, NB, LA, LB, LBN, XSQ, YSQ, GM, GS, FX, GX, FL, GL, GH, FO, LO, FP, FM, LAM, TOP, RHO, EA, EAR, EB, BADR, BADC,
+            XT, XR, Y8, YM, S, PB, VB, UB, ZB, AA, OWN_B, NA, NB, LA, LB, LBN, XSQ, YSQ, GM, GS, FX, GX, FL, GL, GH, FO, FP, FM, LAM, TOP, RHO, EA, EAR, EB, BADR, BADC,
             hsem, ysem, xsem, asem, nsem, fs, fr, gs, gr, ends,
         )
 
 
+def objective(FL, GL):
+    return jnp.sum(jnp.sum(FL[...], axis=0), axis=(0, 1), keepdims=True) + jnp.sum(
+        jnp.sum(GL[...], axis=0), axis=(0, 1), keepdims=True
+    )
+
+
 def work(
     fast, co, row, col, xy, zed, xy_peers, z_peers, across, sibling, own, f_out, g_out, loss_out,
-    XT, XR, Y8, YM, S, PB, VB, UB, ZB, AA, OWN_B, NA, NB, LA, LB, LBN, XSQ, YSQ, GM, GS, FX, GX, FL, GL, GH, FO, LO, FP, FM, LAM, TOP, RHO, EA, EAR, EB, BADR, BADC,
+    XT, XR, Y8, YM, S, PB, VB, UB, ZB, AA, OWN_B, NA, NB, LA, LB, LBN, XSQ, YSQ, GM, GS, FX, GX, FL, GL, GH, FO, FP, FM, LAM, TOP, RHO, EA, EAR, EB, BADR, BADC,
     hsem, ysem, xsem, asem, nsem, fs, fr, gs, gr, ends,
 ):
     other = co["z"] * 4 + across["xl"] * 2
@@ -465,10 +472,14 @@
     GH[co["xl"]] = g
     for t in xy_peers:
         send(GL.at[xy], GL.at[xy], ends.at[0], ends.at[1], t)
+        send(GL.at[xy], GL.at[xy], ends.at[8], ends.at[1], t | {"c": 0})
+    send(GL.at[xy], GL.at[xy], ends.at[8], ends.at[1], sibling)
     send(GH.at[co["xl"]], GH.at[co["xl"]], ends.at[2], ends.at[3], across)
     FL[zed] = jnp.where(bad, jnp.nan, jnp.sum(jnp.exp2(LA[...]) * f, axis=0, keepdims=True))
     for t in z_peers:
         send(FL.at[zed], FL.at[zed], ends.at[10], ends.at[11], t)
+        send(FL.at[zed], FL.at[zed], ends.at[9], ends.at[11], t | {"c": 0})
+    send(FL.at[zed], FL.at[zed], ends.at[9], ends.at[11], sibling)
     FO[...] = jnp.where(co["xl"] == 0, f[0:4], f[8:12])
     send(FO, FO, ends.at[4], ends.at[5], sibling)
     f_out[...] = jnp.where(co["xl"] == 0, f[4:8], f[12:16])
@@ -478,18 +489,14 @@
     g_out[KT:] = GH[1]
     drain(FL.at[pl.ds(0, 7)], ends.at[11])
     drain(GL.at[pl.ds(0, 15)], ends.at[1])
-    loss = jnp.sum(jnp.sum(FL[...], axis=0), axis=(0, 1), keepdims=True) + jnp.sum(
-        jnp.sum(GL[...], axis=0), axis=(0, 1), keepdims=True
-    )
-    LO[...] = jnp.broadcast_to(loss, (1, 128))
-    send(LO, LO, ends.at[8], ends.at[9], sibling)
-    loss_out[...] = loss
+    loss_out[...] = objective(FL, GL)
 
     drain(GL.at[pl.ds(0, 15)], ends.at[0])
     drain(GH.at[0], ends.at[2])
     drain(FO, ends.at[4])
     drain(GH, ends.at[6])
-    drain(LO, ends.at[8])
+    drain(GL, ends.at[8])
+    drain(FL, ends.at[9])
     drain(FL.at[pl.ds(0, 7)], ends.at[10])
     for t in range(ITERS):
         drain(FX.at[t, :, pl.ds(0, 15)], fs.at[t])
@@ -543,7 +550,6 @@
             pltpu.VMEM((16, 1, 128), f32),
             pltpu.VMEM((2, KT, 128), f32),
             pltpu.VMEM((4, 128), f32),
-            pltpu.VMEM((1, 128), f32),
             pltpu.VMEM((ROWS, 128), f32),
             pltpu.VMEM((ROWS, 128), f32),
             pltpu.VMEM((16, 128), f32),

time: 138 us -> 136 us (0.986)
  Pallas kernels: 133 us -> 131 us
    pallas_call x2, Pallas kernels: 133 us -> 131 us  [whole(): pl.pallas_call(functools.partial(kernel, fast), out_shape=(jax.ShapeDtype...]
where the time goes in v9:
time: 136 us
  Pallas kernels  131 us (96%)
  between operations  2.9 us (2%)
  local copies, waits for them, and re-layouts  1.87 us (1%)
    pallas_call x2, Pallas kernels, whole(): pl.pallas_call(functools.partial(kernel, fast), out_shape=(jax.ShapeDtype...  131 us

profile of v9, /device:TPU:1, one launch (start us, length us, event | category | flops | bytes accessed | tf_op | source)
XLA Modules:
  0.0 136.2 jit_solution(9445912404547828972)
XLA Ops:
  0.6 65.8 %sinkhorn.1 = (f32[4,128]{1,0:T(4,128)}, f32[24,128]{1,0:T(8,128)}, f32[1,1]{1,0:T(1,128)}) custom-call(bf16[32,512]{1,0:T(8,128)(2,1)} %bitcast.14, bf16[8,3072]{1,0:T(8,128)(2,1)} %bitcast.12, f32[4,128]{1,0:T(4,128)} %bitcast.19, f32[24,128]{1,0:T(8,128)} %bitcast.16), custom_call_target="tpu_custom_call" | custom-call | tf_op jit(solution)/shard_map/sinkhorn/pallas_call | solution.py:517
  67.0 65.6 %conditional.1 = (f32[]{:T(128)}, f32[4,128]{1,0:T(4,128)}, f32[24,128]{1,0:T(8,128)}) conditional(s32[]{:T(128)} %convert_element_type.3, (bf16[512,32]{0,1:T(8,128)(2,1)}, bf16[3072,8]{0,1:T(8,128)(2,1)}, f32[512]{0:T(512)}, f32[3072]{0:T(1024)}) %tuple.16, (f32[4,128]{1,0:T(4,128)}, f32[24,128]{1,0:T(8,128)}, f32[]{:T(128)}) %tuple.17), branch_computations={%region_0.0_spmd, %region_1.0_spmd} | conditional | bytes 24 | solution.py:586
  67.0 65.6 %sinkhorn_log.1 = (f32[4,128]{1,0:T(4,128)}, f32[24,128]{1,0:T(8,128)}, f32[1,1]{1,0:T(1,128)}) custom-call(bf16[32,512]{1,0:T(8,128)(2,1)} %bitcast.15, bf16[8,3072]{1,0:T(8,128)(2,1)} %bitcast.13, f32[4,128]{1,0:T(4,128)} %bitcast.20, f32[24,128]{1,0:T(8,128)} %bitcast.17), custom_call_target="tpu_custom_call" | custom-call | tf_op jit(solution)/shard_map/cond/branch_0_fun/sinkhorn_log/pallas_call | solution.py:517
  132.6 0.0 copy-start
  132.7 1.3 copy.16
  133.9 0.0 copy-done
  133.9 0.6 copy.17
Async XLA Ops:
  132.6 1.3 copy-start
